TPU v7x, 32 devices: a whole 2x2x4 slice. The times are simulated.
32 devices in a mesh: blk: 8 (over y, x, core), sub: 4 (over z).
Axes of the slice: x: 2, y: 2, z: 4, core: 2. Of those that a mesh axis runs over, the one named last changes fastest.
Arguments:
- features: float32 [1024, 512], P(('blk', 'sub')), may hold values from -3 to 3
- lengthscale: float32 [512], replicated, may hold values from 0.7 to 1.4
- probes: float32 [1024, 64], P(('blk', 'sub')), may hold values from -6 to 6
- cotangent: float32 [1024, 64], P(('blk', 'sub')), may hold values from -1.5 to 1.5
Outputs:
- product: float32 [1024, 64], P(('blk', 'sub'))
- scaled_grad: float32 [1024, 512], P(('blk', 'sub'))
All inputs are finite; a program needn't handle non-finite values.
Results may differ from a plain program's by a relative error of at most 0.0003.
Values sent between devices are 32-bit elements; how exact they have to be, the bound alone decides.
No kernel may reach another device: no remote copies, remote signals or barrier semaphores. Data moves between devices by JAX's collectives and lax.ppermute only.
A program may use at most 64 MiB of HBM per device.

v0:
```python
import jax
import jax.numpy as jnp
from jax import lax
from jax.sharding import PartitionSpec as P

HIGH = lax.Precision.HIGHEST
ROWS_RULE = (((1,), (1,)), ((), ()))
COLS_RULE = (((0,), (0,)), ((), ()))


def passed_along(value, axis, by):
    length = lax.axis_size(axis)
    return lax.ppermute(value, axis, [(i, (i + by) % length) for i in range(length)])


def pair_terms(home_scaled, home_pair, home_norms, away_scaled, away_pair, away_norms):
    middle = away_pair.shape[1] // 2
    inner = lax.dot_general(
        home_scaled, away_scaled, ROWS_RULE, precision=HIGH, preferred_element_type=jnp.float32
    )
    kernel = jnp.exp(-0.5 * (home_norms[:, None] + away_norms[None, :] - 2.0 * inner))
    swapped = jnp.concatenate([away_pair[:, middle:], away_pair[:, :middle]], axis=1)
    cross = lax.dot_general(
        home_pair, swapped, ROWS_RULE, precision=HIGH, preferred_element_type=jnp.float32
    )
    return (kernel, kernel * cross)


def resident_side(kernel, weight, home_scaled, away_scaled, away_pair):
    middle = away_pair.shape[1] // 2
    product = jnp.dot(
        kernel, away_pair[:, :middle], precision=HIGH, preferred_element_type=jnp.float32
    )
    gradient = jnp.dot(weight, away_scaled, precision=HIGH, preferred_element_type=jnp.float32)
    return (product, gradient - jnp.sum(weight, axis=1)[:, None] * home_scaled)


def travel_side(kernel, weight, home_scaled, home_pair, away_scaled):
    middle = home_pair.shape[1] // 2
    product = lax.dot_general(
        kernel, home_pair[:, :middle], COLS_RULE, precision=HIGH, preferred_element_type=jnp.float32
    )
    gradient = lax.dot_general(
        weight, home_scaled, COLS_RULE, precision=HIGH, preferred_element_type=jnp.float32
    )
    return (product, gradient - jnp.sum(weight, axis=0)[:, None] * away_scaled)


def advance(away_scaled, away_pair, away_norms, away_product, away_gradient):
    return passed_along((away_scaled, away_pair, away_norms, away_product, away_gradient), "blk", 1)


def on_device(features, lengthscale, probes, cotangent):
    scaled = features / lengthscale[None, :]
    pairs = jnp.concatenate([probes, cotangent], axis=1)
    norms = jnp.sum(scaled * scaled, axis=1)
    home_scaled, home_pair, home_norms = (
        lax.all_gather(scaled, "sub", axis=0, tiled=True),
        lax.all_gather(pairs, "sub", axis=0, tiled=True),
        lax.all_gather(norms, "sub", axis=0, tiled=True),
    )
    kernel, weight = pair_terms(home_scaled, home_pair, home_norms, scaled, pairs, norms)
    home_product, home_gradient = resident_side(kernel, weight, home_scaled, scaled, pairs)
    blocks = lax.axis_size("blk")
    middle = blocks // 2

    def step_two(offset, running):
        moved = advance(running[0], running[1], running[2], running[3], running[4])
        kernel_now, weight_now = pair_terms(
            home_scaled, home_pair, home_norms, moved[0], moved[1], moved[2]
        )
        near_product, near_gradient = resident_side(
            kernel_now, weight_now, home_scaled, moved[0], moved[1]
        )
        far_product, far_gradient = travel_side(
            kernel_now, weight_now, home_scaled, home_pair, moved[0]
        )
        return (
            moved[0],
            moved[1],
            moved[2],
            moved[3] + far_product,
            moved[4] + far_gradient,
            running[5] + near_product,
            running[6] + near_gradient,
        )

    start = (
        scaled,
        pairs,
        norms,
        jnp.zeros(probes.shape, jnp.float32),
        jnp.zeros(features.shape, jnp.float32),
        home_product,
        home_gradient,
    )
    running = lax.fori_loop(1, middle, step_two, start)
    moved = advance(running[0], running[1], running[2], running[3], running[4])
    kernel_last, weight_last = pair_terms(
        home_scaled, home_pair, home_norms, moved[0], moved[1], moved[2]
    )
    last_product, last_gradient = resident_side(
        kernel_last, weight_last, home_scaled, moved[0], moved[1]
    )
    home_product = running[5] + last_product
    home_gradient = running[6] + last_gradient
    back_product, back_gradient = passed_along((moved[3], moved[4]), "blk", middle)
    own_product, own_gradient = (
        lax.psum_scatter(home_product, "sub", scatter_dimension=0, tiled=True),
        lax.psum_scatter(home_gradient, "sub", scatter_dimension=0, tiled=True),
    )
    return (own_product + back_product, own_gradient + back_gradient)


def solution(mesh):
    in_specs = (P(("blk", "sub"), None), P(), P(("blk", "sub"), None), P(("blk", "sub"), None))
    out_specs = (P(("blk", "sub"), None), P(("blk", "sub"), None))
    return jax.shard_map(
        on_device, mesh=mesh, in_specs=in_specs, out_specs=out_specs, check_vma=False
    )
```

profile of v0, /device:TPU:0, one launch (start us, length us, event | category | flops | bytes accessed | tf_op | source)
XLA Modules:
  0.0 133.9 jit_solution(16144356869923501800)
XLA Ops:
  7.2 0.8 pad_maximum_fusion
  8.1 14.9 %all_gather.11 = f32[128,128]{1,0:T(8,128)S(1)} all-gather(f32[32,128]{1,0:T(8,128)S(1)} %pad_maximum_fusion), channel_id=1, replica_groups=mesh['blk'=8,'sub'=4] {'sub'}, dimensions={0}, use_global_device_ids=true | all-gather | bytes 81920 | tf_op jit(solution)/shard_map/all_gather | solution.py:59
  23.0 0.7 copy-done.4
  23.6 0.6 dynamic-slice
  25.3 11.8 %all-reduce = f32[128]{0:T(128)S(1)} all-reduce(f32[128]{0:T(128)S(1)} %dynamic-update-slice), channel_id=1, replica_groups=mesh['blk'=8,'sub'=4] {'sub'}, use_global_device_ids=true, to_apply=%add | all-reduce | flops 128 | bytes 1024
  37.1 14.1 %all_gather.10 = f32[128,512]{1,0:T(8,128)S(1)} all-gather(f32[32,512]{1,0:T(8,128)S(1)} %get-tuple-element.221), channel_id=1, replica_groups=mesh['blk'=8,'sub'=4] {'sub'}, dimensions={0}, use_global_device_ids=true | all-gather | bytes 327680 | tf_op jit(solution)/shard_map/all_gather | solution.py:58
  53.3 28.8 %while.23 = (s32[]{:T(128)}, f32[32,512]{1,0:T(8,128)S(1)}, f32[32,128]{1,0:T(8,128)S(1)}, f32[32]{0:T(128)S(1)}, f32[32,64]{1,0:T(8,128)S(1)}, /*index=5*/f32[3...) while((s32[]{:T(128)}, f32[32,512]{1,0:T(8,128)S(1)}, ...), condition=%wide.region_5.0_spmd.clone, body=%wide.region_2.0_spmd.clone.sunk | while | flops 88412000 | bytes 2969808 | solution.py:97
  53.4 1.6 %collective-permute-start.3 = (f32[32,64]{1,0:T(8,128)S(1)}, f32[32,64]{1,0:T(8,128)S(1)}, u32[]{:S(2)}, u32[]{:S(2)}) collective-permute-start(f32[32,64]{1,0:T(8,128)S(1)} %broadcast_select_fusion.4), channel_id=1, source_target_pairs={{0,4},{4,8},{8,12},{12,16},{16,20},{20,24},{24,28},{28,0},{1,5},{5... | collective-permute-start | bytes 24584 | tf_op jit(solution)/shard_map/while/body/eval_jaxpr/ppermute | solution.py:13
  55.1 1.6 %collective-permute-start.4 = (f32[32,512]{1,0:T(8,128)S(1)}, f32[32,512]{1,0:T(8,128)S(1)}, u32[]{:S(2)}, u32[]{:S(2)}) collective-permute-start(f32[32,512]{1,0:T(8,128)S(1)} %broadcast_select_fusion.5), channel_id=1, source_target_pairs={{0,4},{4,8},{8,12},{12,16},{16,20},{20,24},{24,28},{28,0},{1,5},{5... | collective-permute-start | bytes 196616 | tf_op jit(solution)/shard_map/while/body/eval_jaxpr/ppermute | solution.py:13
  57.2 1.8 %collective-permute-done.1 = f32[32,128]{1,0:T(8,128)S(1)} collective-permute-done((f32[32,128]{1,0:T(8,128)S(1)}, f32[32,128]{1,0:T(8,128)S(1)}, u32[]{:S(2)}, u32[]{:S(2)}) %collective-permute-start.1) | collective-permute-done | bytes 16416 | tf_op jit(solution)/shard_map/while/body/eval_jaxpr/ppermute | solution.py:13
  59.1 2.1 %collective-permute-done = f32[32,512]{1,0:T(8,128)S(1)} collective-permute-done((f32[32,512]{1,0:T(8,128)S(1)}, f32[32,512]{1,0:T(8,128)S(1)}, u32[]{:S(2)}, u32[]{:S(2)}) %collective-permute-start) | collective-permute-done | bytes 65568 | tf_op jit(solution)/shard_map/while/body/eval_jaxpr/ppermute | solution.py:13
  63.4 0.7 collective-permute-start.3
  64.1 1.7 %collective-permute-start.4 = (f32[32,512]{1,0:T(8,128)S(1)}, f32[32,512]{1,0:T(8,128)S(1)}, u32[]{:S(2)}, u32[]{:S(2)}) collective-permute-start(f32[32,512]{1,0:T(8,128)S(1)} %broadcast_select_fusion.5), channel_id=1, source_target_pairs={{0,4},{4,8},{8,12},{12,16},{16,20},{20,24},{24,28},{28,0},{1,5},{5... | collective-permute-start | bytes 196616 | tf_op jit(solution)/shard_map/while/body/eval_jaxpr/ppermute | solution.py:13
  65.9 1.3 collective-permute-done.2
  67.2 0.9 collective-permute-done.1
  68.2 2.2 %collective-permute-done = f32[32,512]{1,0:T(8,128)S(1)} collective-permute-done((f32[32,512]{1,0:T(8,128)S(1)}, f32[32,512]{1,0:T(8,128)S(1)}, u32[]{:S(2)}, u32[]{:S(2)}) %collective-permute-start) | collective-permute-done | bytes 65568 | tf_op jit(solution)/shard_map/while/body/eval_jaxpr/ppermute | solution.py:13
  72.7 2.9 %collective-permute-start.4 = (f32[32,512]{1,0:T(8,128)S(1)}, f32[32,512]{1,0:T(8,128)S(1)}, u32[]{:S(2)}, u32[]{:S(2)}) collective-permute-start(f32[32,512]{1,0:T(8,128)S(1)} %broadcast_select_fusion.5), channel_id=1, source_target_pairs={{0,4},{4,8},{8,12},{12,16},{16,20},{20,24},{24,28},{28,0},{1,5},{5... | collective-permute-start | bytes 196616 | tf_op jit(solution)/shard_map/while/body/eval_jaxpr/ppermute | solution.py:13
  75.6 0.7 collective-permute-done.2
  76.9 3.2 %collective-permute-done = f32[32,512]{1,0:T(8,128)S(1)} collective-permute-done((f32[32,512]{1,0:T(8,128)S(1)}, f32[32,512]{1,0:T(8,128)S(1)}, u32[]{:S(2)}, u32[]{:S(2)}) %collective-permute-start) | collective-permute-done | bytes 65568 | tf_op jit(solution)/shard_map/while/body/eval_jaxpr/ppermute | solution.py:13
  82.5 3.8 %collective-permute-done.7 = f32[32,128]{1,0:T(8,128)S(1)} collective-permute-done((f32[32,128]{1,0:T(8,128)S(1)}, f32[32,128]{1,0:T(8,128)S(1)}, u32[]{:S(2)}, u32[]{:S(2)}) %collective-permute-start.7) | collective-permute-done | bytes 16416 | tf_op jit(solution)/shard_map/ppermute | solution.py:13
  86.4 0.6 collective-permute-done.6
  87.4 1.0 convolution_add_fusion.2
  88.7 1.1 fusion.16
  89.9 4.6 %collective-permute-done.10 = f32[32,512]{1,0:T(8,128)S(1)} collective-permute-done((f32[32,512]{1,0:T(8,128)S(1)}, f32[32,512]{1,0:T(8,128)S(1)}, u32[]{:S(2)}, u32[]{:S(2)}) %collective-permute-start.10) | collective-permute-done | bytes 65568 | tf_op jit(solution)/shard_map/ppermute | solution.py:13
  94.5 0.7 collective-permute-start.11
  95.3 4.1 %collective-permute-done.8 = f32[32,64]{1,0:T(8,128)S(1)} collective-permute-done((f32[32,64]{1,0:T(8,128)S(1)}, f32[32,64]{1,0:T(8,128)S(1)}, u32[]{:S(2)}, u32[]{:S(2)}) %collective-permute-start.8) | collective-permute-done | bytes 8224 | tf_op jit(solution)/shard_map/ppermute | solution.py:13
  99.3 1.3 collective-permute-start.9
  100.6 2.4 %collective-permute-done.9 = f32[32,64]{1,0:T(8,128)S(1)} collective-permute-done((f32[32,64]{1,0:T(8,128)S(1)}, f32[32,64]{1,0:T(8,128)S(1)}, u32[]{:S(2)}, u32[]{:S(2)}) %collective-permute-start.9) | collective-permute-done | bytes 8224 | tf_op jit(solution)/shard_map/ppermute | solution.py:13
  103.1 2.3 %reduce-scatter.3.cloned.1.call-done = f32[32,64]{1,0:T(8,128)} async-done(((f32[128,64]{1,0:T(8,128)}), f32[32,64]{1,0:T(8,128)}) %reduce-scatter.3.cloned.1.call-update) | async-done | bytes 8208 | tf_op jit(solution)/shard_map/reduce_scatter | solution.py:109
  105.4 1.3 add.74
  106.7 18.8 %reduce-scatter.5.cloned.1.call-done = f32[32,512]{1,0:T(8,128)} async-done(((f32[128,512]{1,0:T(8,128)}), f32[32,512]{1,0:T(8,128)}) %reduce-scatter.5.cloned.1.call-update) | async-done | bytes 65552 | tf_op jit(solution)/shard_map/reduce_scatter | solution.py:110
  125.5 1.5 %add.76 = f32[32,512]{1,0:T(8,128)} add(f32[32,512]{1,0:T(8,128)} %reduce-scatter.5.cloned.1.call-done, f32[32,512]{1,0:T(8,128)S(1)} %collective-permute-done.11) | non-fusion elementwise | flops 16384 | bytes 196608 | tf_op jit(solution)/shard_map/add | solution.py:112
  (87 shorter events, 11.4 us)
Async XLA Ops:
  7.2 98.2 %reduce-scatter.3.cloned.1.call-start = ((), (), s32[]{:S(2)}) async-start(), calls=%async_computation.2 | async-start | bytes 81920 | tf_op jit(solution)/shard_map/reduce_scatter | solution.py:109
  7.2 17.6 %copy-start.1 = (f32[32,512]{1,0:T(8,128)S(1)}, f32[32,512]{1,0:T(8,128)}, u32[]{:S(2)}) copy-start(f32[32,512]{1,0:T(8,128)} %param.6) | copy-start | bytes 196612
  23.0 0.7 copy-start.4
  23.6 1.2 copy-start.3
  51.2 0.7 copy-start
  51.9 0.7 copy-start.2
  53.3 3.9 %collective-permute-start.2 = (f32[32]{0:T(128)S(1)}, f32[32]{0:T(128)S(1)}, u32[]{:S(2)}, u32[]{:S(2)}) collective-permute-start(f32[32]{0:T(128)S(1)} %get-tuple-element.236), channel_id=1, source_target_pairs={{0,4},{4,8},{8,12},{12,16},{16,20},{20,24},{24,28},{28,0},{1,5},{5... | collective-permute-start | bytes 392 | tf_op jit(solution)/shard_map/while/body/eval_jaxpr/ppermute | solution.py:13
  53.4 8.5 %collective-permute-start.3 = (f32[32,64]{1,0:T(8,128)S(1)}, f32[32,64]{1,0:T(8,128)S(1)}, u32[]{:S(2)}, u32[]{:S(2)}) collective-permute-start(f32[32,64]{1,0:T(8,128)S(1)} %broadcast_select_fusion.4), channel_id=1, source_target_pairs={{0,4},{4,8},{8,12},{12,16},{16,20},{20,24},{24,28},{28,0},{1,5},{5... | collective-permute-start | bytes 24584 | tf_op jit(solution)/shard_map/while/body/eval_jaxpr/ppermute | solution.py:13
  55.0 4.1 %collective-permute-start.1 = (f32[32,128]{1,0:T(8,128)S(1)}, f32[32,128]{1,0:T(8,128)S(1)}, u32[]{:S(2)}, u32[]{:S(2)}) collective-permute-start(f32[32,128]{1,0:T(8,128)S(1)} %get-tuple-element.235), channel_id=1, source_target_pairs={{0,4},{4,8},{8,12},{12,16},{16,20},{20,24},{24,28},{28,0},{1,5},{5... | collective-permute-start | bytes 49160 | tf_op jit(solution)/shard_map/while/body/eval_jaxpr/ppermute | solution.py:13
  55.1 7.4 %collective-permute-start.4 = (f32[32,512]{1,0:T(8,128)S(1)}, f32[32,512]{1,0:T(8,128)S(1)}, u32[]{:S(2)}, u32[]{:S(2)}) collective-permute-start(f32[32,512]{1,0:T(8,128)S(1)} %broadcast_select_fusion.5), channel_id=1, source_target_pairs={{0,4},{4,8},{8,12},{12,16},{16,20},{20,24},{24,28},{28,0},{1,5},{5... | collective-permute-start | bytes 196616 | tf_op jit(solution)/shard_map/while/body/eval_jaxpr/ppermute | solution.py:13
  56.7 4.6 %collective-permute-start = (f32[32,512]{1,0:T(8,128)S(1)}, f32[32,512]{1,0:T(8,128)S(1)}, u32[]{:S(2)}, u32[]{:S(2)}) collective-permute-start(f32[32,512]{1,0:T(8,128)S(1)} %get-tuple-element.234), channel_id=1, source_target_pairs={{0,4},{4,8},{8,12},{12,16},{16,20},{20,24},{24,28},{28,0},{1,5},{5... | collective-permute-start | bytes 196616 | tf_op jit(solution)/shard_map/while/body/eval_jaxpr/ppermute | solution.py:13
  63.3 3.9 %collective-permute-start.2 = (f32[32]{0:T(128)S(1)}, f32[32]{0:T(128)S(1)}, u32[]{:S(2)}, u32[]{:S(2)}) collective-permute-start(f32[32]{0:T(128)S(1)} %get-tuple-element.236), channel_id=1, source_target_pairs={{0,4},{4,8},{8,12},{12,16},{16,20},{20,24},{24,28},{28,0},{1,5},{5... | collective-permute-start | bytes 392 | tf_op jit(solution)/shard_map/while/body/eval_jaxpr/ppermute | solution.py:13
  63.4 7.7 %collective-permute-start.3 = (f32[32,64]{1,0:T(8,128)S(1)}, f32[32,64]{1,0:T(8,128)S(1)}, u32[]{:S(2)}, u32[]{:S(2)}) collective-permute-start(f32[32,64]{1,0:T(8,128)S(1)} %broadcast_select_fusion.4), channel_id=1, source_target_pairs={{0,4},{4,8},{8,12},{12,16},{16,20},{20,24},{24,28},{28,0},{1,5},{5... | collective-permute-start | bytes 24584 | tf_op jit(solution)/shard_map/while/body/eval_jaxpr/ppermute | solution.py:13
  64.1 4.1 %collective-permute-start.1 = (f32[32,128]{1,0:T(8,128)S(1)}, f32[32,128]{1,0:T(8,128)S(1)}, u32[]{:S(2)}, u32[]{:S(2)}) collective-permute-start(f32[32,128]{1,0:T(8,128)S(1)} %get-tuple-element.235), channel_id=1, source_target_pairs={{0,4},{4,8},{8,12},{12,16},{16,20},{20,24},{24,28},{28,0},{1,5},{5... | collective-permute-start | bytes 49160 | tf_op jit(solution)/shard_map/while/body/eval_jaxpr/ppermute | solution.py:13
  64.1 7.5 %collective-permute-start.4 = (f32[32,512]{1,0:T(8,128)S(1)}, f32[32,512]{1,0:T(8,128)S(1)}, u32[]{:S(2)}, u32[]{:S(2)}) collective-permute-start(f32[32,512]{1,0:T(8,128)S(1)} %broadcast_select_fusion.5), channel_id=1, source_target_pairs={{0,4},{4,8},{8,12},{12,16},{16,20},{20,24},{24,28},{28,0},{1,5},{5... | collective-permute-start | bytes 196616 | tf_op jit(solution)/shard_map/while/body/eval_jaxpr/ppermute | solution.py:13
  65.8 4.6 %collective-permute-start = (f32[32,512]{1,0:T(8,128)S(1)}, f32[32,512]{1,0:T(8,128)S(1)}, u32[]{:S(2)}, u32[]{:S(2)}) collective-permute-start(f32[32,512]{1,0:T(8,128)S(1)} %get-tuple-element.234), channel_id=1, source_target_pairs={{0,4},{4,8},{8,12},{12,16},{16,20},{20,24},{24,28},{28,0},{1,5},{5... | collective-permute-start | bytes 196616 | tf_op jit(solution)/shard_map/while/body/eval_jaxpr/ppermute | solution.py:13
  72.5 3.9 %collective-permute-start.2 = (f32[32]{0:T(128)S(1)}, f32[32]{0:T(128)S(1)}, u32[]{:S(2)}, u32[]{:S(2)}) collective-permute-start(f32[32]{0:T(128)S(1)} %get-tuple-element.236), channel_id=1, source_target_pairs={{0,4},{4,8},{8,12},{12,16},{16,20},{20,24},{24,28},{28,0},{1,5},{5... | collective-permute-start | bytes 392 | tf_op jit(solution)/shard_map/while/body/eval_jaxpr/ppermute | solution.py:13
  72.5 8.2 %collective-permute-start.3 = (f32[32,64]{1,0:T(8,128)S(1)}, f32[32,64]{1,0:T(8,128)S(1)}, u32[]{:S(2)}, u32[]{:S(2)}) collective-permute-start(f32[32,64]{1,0:T(8,128)S(1)} %broadcast_select_fusion.4), channel_id=1, source_target_pairs={{0,4},{4,8},{8,12},{12,16},{16,20},{20,24},{24,28},{28,0},{1,5},{5... | collective-permute-start | bytes 24584 | tf_op jit(solution)/shard_map/while/body/eval_jaxpr/ppermute | solution.py:13
  72.6 4.2 %collective-permute-start.1 = (f32[32,128]{1,0:T(8,128)S(1)}, f32[32,128]{1,0:T(8,128)S(1)}, u32[]{:S(2)}, u32[]{:S(2)}) collective-permute-start(f32[32,128]{1,0:T(8,128)S(1)} %get-tuple-element.235), channel_id=1, source_target_pairs={{0,4},{4,8},{8,12},{12,16},{16,20},{20,24},{24,28},{28,0},{1,5},{5... | collective-permute-start | bytes 49160 | tf_op jit(solution)/shard_map/while/body/eval_jaxpr/ppermute | solution.py:13
  72.7 8.7 %collective-permute-start.4 = (f32[32,512]{1,0:T(8,128)S(1)}, f32[32,512]{1,0:T(8,128)S(1)}, u32[]{:S(2)}, u32[]{:S(2)}) collective-permute-start(f32[32,512]{1,0:T(8,128)S(1)} %broadcast_select_fusion.5), channel_id=1, source_target_pairs={{0,4},{4,8},{8,12},{12,16},{16,20},{20,24},{24,28},{28,0},{1,5},{5... | collective-permute-start | bytes 196616 | tf_op jit(solution)/shard_map/while/body/eval_jaxpr/ppermute | solution.py:13
  75.6 4.6 %collective-permute-start = (f32[32,512]{1,0:T(8,128)S(1)}, f32[32,512]{1,0:T(8,128)S(1)}, u32[]{:S(2)}, u32[]{:S(2)}) collective-permute-start(f32[32,512]{1,0:T(8,128)S(1)} %get-tuple-element.234), channel_id=1, source_target_pairs={{0,4},{4,8},{8,12},{12,16},{16,20},{20,24},{24,28},{28,0},{1,5},{5... | collective-permute-start | bytes 196616 | tf_op jit(solution)/shard_map/while/body/eval_jaxpr/ppermute | solution.py:13
  82.2 4.1 %collective-permute-start.7 = (f32[32,128]{1,0:T(8,128)S(1)}, f32[32,128]{1,0:T(8,128)S(1)}, u32[]{:S(2)}, u32[]{:S(2)}) collective-permute-start(f32[32,128]{1,0:T(8,128)S(1)} %get-tuple-element.68), channel_id=1, source_target_pairs={{0,4},{4,8},{8,12},{12,16},{16,20},{20,24},{24,28},{28,0},{1,5},{5... | collective-permute-start | bytes 49160 | tf_op jit(solution)/shard_map/ppermute | solution.py:13
  82.2 5.1 %collective-permute-start.5 = (f32[32]{0:T(128)S(1)}, f32[32]{0:T(128)S(1)}, u32[]{:S(2)}, u32[]{:S(2)}) collective-permute-start(f32[32]{0:T(128)S(1)} %get-tuple-element.66), channel_id=1, source_target_pairs={{0,4},{4,8},{8,12},{12,16},{16,20},{20,24},{24,28},{28,0},{1,5},{5... | collective-permute-start | bytes 392 | tf_op jit(solution)/shard_map/ppermute | solution.py:13
  82.3 4.7 %collective-permute-start.6 = (f32[32,512]{1,0:T(8,128)S(1)}, f32[32,512]{1,0:T(8,128)S(1)}, u32[]{:S(2)}, u32[]{:S(2)}) collective-permute-start(f32[32,512]{1,0:T(8,128)S(1)} %get-tuple-element.67), channel_id=1, source_target_pairs={{0,4},{4,8},{8,12},{12,16},{16,20},{20,24},{24,28},{28,0},{1,5},{5... | collective-permute-start | bytes 196616 | tf_op jit(solution)/shard_map/ppermute | solution.py:13
  88.4 37.2 %reduce-scatter.5.cloned.1.call-start = ((), (), s32[]{:S(2)}) async-start(), calls=%async_computation.3 | async-start | bytes 327680 | tf_op jit(solution)/shard_map/reduce_scatter | solution.py:110
  89.9 4.6 %collective-permute-start.10 = (f32[32,512]{1,0:T(8,128)S(1)}, f32[32,512]{1,0:T(8,128)S(1)}, u32[]{:S(2)}, u32[]{:S(2)}) collective-permute-start(f32[32,512]{1,0:T(8,128)S(1)} %get-tuple-element.71), channel_id=1, source_target_pairs={{0,4},{4,8},{8,12},{12,16},{16,20},{20,24},{24,28},{28,0},{1,5},{5... | collective-permute-start | bytes 196616 | tf_op jit(solution)/shard_map/ppermute | solution.py:13
  94.5 12.2 %collective-permute-start.11 = (f32[32,512]{1,0:T(8,128)S(1)}, f32[32,512]{1,0:T(8,128)S(1)}, u32[]{:S(2)}, u32[]{:S(2)}) collective-permute-start(f32[32,512]{1,0:T(8,128)S(1)} %collective-permute-done.10), channel_id=1, source_target_pairs={{0,16},{4,20},{8,24},{12,28},{16,0},{20,4},{24,8},{28,12},{1,17},{... | collective-permute-start | bytes 196616 | tf_op jit(solution)/shard_map/ppermute | solution.py:13
  95.3 4.1 %collective-permute-start.8 = (f32[32,64]{1,0:T(8,128)S(1)}, f32[32,64]{1,0:T(8,128)S(1)}, u32[]{:S(2)}, u32[]{:S(2)}) collective-permute-start(f32[32,64]{1,0:T(8,128)S(1)} %get-tuple-element.69), channel_id=1, source_target_pairs={{0,4},{4,8},{8,12},{12,16},{16,20},{20,24},{24,28},{28,0},{1,5},{5... | collective-permute-start | bytes 24584 | tf_op jit(solution)/shard_map/ppermute | solution.py:13
  99.3 3.7 %collective-permute-start.9 = (f32[32,64]{1,0:T(8,128)S(1)}, f32[32,64]{1,0:T(8,128)S(1)}, u32[]{:S(2)}, u32[]{:S(2)}) collective-permute-start(f32[32,64]{1,0:T(8,128)S(1)} %collective-permute-done.8), channel_id=1, source_target_pairs={{0,16},{4,20},{8,24},{12,28},{16,0},{20,4},{24,8},{28,12},{1,17},{... | collective-permute-start | bytes 24584 | tf_op jit(solution)/shard_map/ppermute | solution.py:13
Sparse Core Ops, SparseCore 0:
  88.5 16.8 reduce-scatter.2
  107.7 17.7 reduce-scatter.4
where the time goes:
time: 134 us
  waiting for transfers between devices  50 us (37%)
  blocking collectives  40.8 us (30%)
  between operations  14.8 us (11%)
  starting transfers between devices  11.4 us (9%)
  matrix products  9.89 us (7%)
  other arithmetic  3.81 us (3%)
  local copies, waits for them, and re-layouts  2.72 us (2%)
    ppermute x22, waiting for transfers between devices, passed_along(): lax.ppermute(value, axis, [(i, (i + by) % length) for i in range(length)])  28.8 us
    reduce_scatter x1, waiting for transfers between devices, on_device(): lax.psum_scatter(home_gradient, 'sub', scatter_dimension=0, tiled=True)  18.8 us
    all_gather x1, blocking collectives, on_device(): lax.all_gather(pairs, 'sub', axis=0, tiled=True)  14.9 us
    all_gather x1, blocking collectives, on_device(): lax.all_gather(scaled, 'sub', axis=0, tiled=True)  14.1 us
    unnamed x1, blocking collectives  11.8 us
    ppermute x22, starting transfers between devices, passed_along(): lax.ppermute(value, axis, [(i, (i + by) % length) for i in range(length)])  11.4 us
    dot_general x5, matrix products, resident_side(): jnp.dot(weight, away_scaled, precision=HIGH, preferred_element_type=jnp.f...  2.96 us
    add x2, other arithmetic, on_device(): return (own_product + back_product, own_gradient + back_gradient)  2.8 us
  transfers between devices with their start and end apart: 24, of which 16 were waited for; matrix products, arithmetic and copies ran while one was open for 5% of the time, Pallas kernels for 0%

commit v1 on v0

v1 whole, which is shorter than its diff:
```python
import jax
import jax.numpy as jnp
from jax import lax
from jax.sharding import PartitionSpec as P

HIGH = lax.Precision.HIGHEST
ROWS_RULE = (((1,), (1,)), ((), ()))
CORES = 2


def partner(position, step, length):
    if length & (length - 1) == 0:
        return position ^ step
    return (position + step) % length


def over_plane(value, step, back=False):
    blocks = lax.axis_size("blk")
    places = blocks // CORES
    pairs = [
        (p * CORES + c, partner(p, step, places) * CORES + c)
        for p in range(places)
        for c in range(CORES)
    ]
    return lax.ppermute(value, "blk", [(b, a) for a, b in pairs] if back else pairs)


def over_line(value, step):
    length = lax.axis_size("sub")
    return lax.ppermute(value, "sub", [(p, partner(p, step, length)) for p in range(length)])


def over_cores(value):
    return lax.ppermute(value, "blk", [(i, i ^ 1) for i in range(lax.axis_size("blk"))])


def on_device(features, lengthscale, probes, cotangent):
    width, probe_count = features.shape[1], probes.shape[1]
    points = features.shape[0]
    places, length = lax.axis_size("blk") // CORES, lax.axis_size("sub")
    scaled = features / lengthscale[None, :]
    data = jnp.concatenate([scaled, probes, cotangent], axis=1)
    line = [data] + [over_line(data, step) for step in range(length - 1, 0, -1)]
    plane = [data] + [over_plane(data, step) for step in range(places - 1, 0, -1)]
    near = jnp.concatenate(line, axis=0)
    columns = jnp.concatenate([near, over_cores(near)], axis=0)
    rows = jnp.concatenate(plane, axis=0)
    row_scaled, column_scaled = rows[:, :width], columns[:, :width]
    row_norms = jnp.sum(row_scaled * row_scaled, axis=1)
    column_norms = jnp.sum(column_scaled * column_scaled, axis=1)
    inner = lax.dot_general(
        row_scaled, column_scaled, ROWS_RULE, precision=HIGH, preferred_element_type=jnp.float32
    )
    kernel = jnp.exp(-0.5 * (row_norms[:, None] + column_norms[None, :] - 2.0 * inner))
    column_probes = columns[:, width : width + probe_count]
    swapped = jnp.concatenate([columns[:, width + probe_count :], column_probes], axis=1)
    cross = lax.dot_general(
        rows[:, width:], swapped, ROWS_RULE, precision=HIGH, preferred_element_type=jnp.float32
    )
    weight = kernel * cross
    product = jnp.dot(kernel, column_probes, precision=HIGH, preferred_element_type=jnp.float32)
    gradient = jnp.dot(weight, column_scaled, precision=HIGH, preferred_element_type=jnp.float32)
    gradient = gradient - jnp.sum(weight, axis=1)[:, None] * row_scaled
    partial = jnp.concatenate([gradient, product], axis=1)
    total = partial[:points]
    for place, step in enumerate(range(places - 1, 0, -1), 1):
        total = total + over_plane(partial[place * points : (place + 1) * points], step, True)
    return (total[:, width:], total[:, :width])


def solution(mesh):
    spec = P(("blk", "sub"), None)
    return jax.shard_map(
        on_device, mesh=mesh, in_specs=(spec, P(), spec, spec), out_specs=(spec, spec), check_vma=False
    )
```

time: 134 us -> 29.3 us (0.22)
  blocking collectives: 40.8 us -> 0 us
  waiting for transfers between devices: 50 us -> 9.21 us
  between operations: 14.8 us -> 0.76 us
  matrix products: 9.89 us -> 1.81 us
  starting transfers between devices: 11.4 us -> 14.4 us
  other arithmetic: 3.81 us -> 1.28 us
    all_gather x2 -> x0, blocking collectives: 29 us -> none  [the longest x1 14.9 us: on_device(): lax.all_gather(pairs, 'sub', axis=0, tiled=True)]
    reduce_scatter x2 -> x0, waiting for transfers between devices: 21.2 us -> none  [the longest x1 18.8 us: on_device(): lax.psum_scatter(home_gradient, 'sub', scatter_dimension=0, tiled=True)]
    ppermute x22 -> x10, waiting for transfers between devices: 28.8 us -> 9.21 us  [the longest x6 6.63 us: over_plane(): lax.ppermute(value, 'blk', [(b, a) for a, b in pairs] if back else pairs)]
    unnamed x1 -> x0, blocking collectives: 11.8 us -> none
    dot_general x26 -> x4, matrix products: 9.89 us -> 1.81 us  [the longest x1 0.68 us: on_device(): lax.dot_general(row_scaled, column_scaled, ROWS_RULE, precision=HIGH, pre...]
    ppermute x22 -> x10, starting transfers between devices: 11.4 us -> 14.4 us  [the longest x6 8.65 us: over_plane(): lax.ppermute(value, 'blk', [(b, a) for a, b in pairs] if back else pairs)]
    add x2 -> x1, other arithmetic: 2.8 us -> 0.02 us  [on_device(): total + over_plane(partial[place * points:(place + 1) * points], step, True)]
    unnamed x13 -> x7, local copies, waits for them, and re-layouts: 2.31 us -> 0.03 us
  transfers between devices with their start and end apart: 24 -> 10, of which waited for: 16 -> 7; matrix products, arithmetic and copies ran while one was open for 5% -> 0% of each run, Pallas kernels for 0% -> 0%
where the time goes in v1:
time: 29.3 us; the launch traced here: 28.8 us
  starting transfers between devices  14.4 us (49%)
  waiting for transfers between devices  9.21 us (31%)
  matrix products  1.81 us (6%)
  local copies, waits for them, and re-layouts  1.39 us (5%)
  other arithmetic  1.28 us (4%)
  between operations  0.76 us (3%)
    ppermute x6, starting transfers between devices, over_plane(): lax.ppermute(value, 'blk', [(b, a) for a, b in pairs] if back else pairs)  8.65 us
    ppermute x6, waiting for transfers between devices, over_plane(): lax.ppermute(value, 'blk', [(b, a) for a, b in pairs] if back else pairs)  6.63 us
    ppermute x3, starting transfers between devices, over_line(): lax.ppermute(value, 'sub', [(p, partner(p, step, length)) for p in range(...  5.7 us
    ppermute x1, waiting for transfers between devices, over_cores(): lax.ppermute(value, 'blk', [(i, i ^ 1) for i in range(lax.axis_size('blk'...  1.46 us
    slice x2, local copies, waits for them, and re-layouts, on_device(): return (total[:, width:], total[:, :width])  1.24 us
    ppermute x3, waiting for transfers between devices, over_line(): lax.ppermute(value, 'sub', [(p, partner(p, step, length)) for p in range(...  1.13 us
    div x1, other arithmetic, on_device(): scaled = features / lengthscale[None, :]  0.86 us
    dot_general x1, matrix products, on_device(): lax.dot_general(row_scaled, column_scaled, ROWS_RULE, precision=HIGH, pre...  0.68 us
  transfers between devices with their start and end apart: 10, of which 7 were waited for; matrix products, arithmetic and copies ran while one was open for 0% of the time, Pallas kernels for 0%

profile of v1, /device:TPU:0, one launch (start us, length us, event | category | flops | bytes accessed | tf_op | source)
XLA Modules:
  0.0 28.8 jit_solution(5852460055264276992)
XLA Ops:
  0.7 0.9 %broadcast_divide_fusion = f32[32,512]{1,0:T(8,128)S(1)} fusion(f32[32,512]{1,0:T(8,128)} %param.4, f32[512]{0:T(512)} %param.5), kind=kLoop, calls=%fused_computation.34 | loop fusion | flops 16384 | bytes 133120 | tf_op jit(solution)/shard_map/div | solution.py:41
  1.5 0.1 constant_dynamic-update-slice_fusion.4
  1.6 5.1 %collective-permute-start.3 = (f32[32,640]{1,0:T(8,128)S(1)}, f32[32,640]{1,0:T(8,128)S(1)}, u32[]{:S(2)}, u32[]{:S(2)}) collective-permute-start(f32[32,640]{1,0:T(8,128)S(1)} %get-tuple-element.3), channel_id=1, source_target_pairs={{0,3},{1,2},{2,1},{3,0},{4,7},{5,6},{6,5},{7,4},{8,11},{9,10},{10,... | collective-permute-start | bytes 245768 | tf_op jit(solution)/shard_map/ppermute | solution.py:30
  6.7 0.0 collective-permute-start.4
  6.7 0.6 %collective-permute-start.5 = (f32[32,640]{1,0:T(8,128)S(1)}, f32[32,640]{1,0:T(8,128)S(1)}, u32[]{:S(2)}, u32[]{:S(2)}) collective-permute-start(f32[32,640]{1,0:T(8,128)S(1)} %get-tuple-element.3), channel_id=1, source_target_pairs={{0,1},{1,0},{2,3},{3,2},{4,5},{5,4},{6,7},{7,6},{8,9},{9,8},{10,11... | collective-permute-start | bytes 245768 | tf_op jit(solution)/shard_map/ppermute | solution.py:30
  7.3 1.6 %collective-permute-start.2 = (f32[32,640]{1,0:T(8,128)S(1)}, f32[32,640]{1,0:T(8,128)S(1)}, u32[]{:S(2)}, u32[]{:S(2)}) collective-permute-start(f32[32,640]{1,0:T(8,128)S(1)} %get-tuple-element.3), channel_id=1, source_target_pairs={{0,8},{4,12},{8,0},{12,4},{16,24},{20,28},{24,16},{28,20},{1,9},{5... | collective-permute-start | bytes 245768 | tf_op jit(solution)/shard_map/ppermute | solution.py:25
  9.0 1.5 %collective-permute-start.1 = (f32[32,640]{1,0:T(8,128)S(1)}, f32[32,640]{1,0:T(8,128)S(1)}, u32[]{:S(2)}, u32[]{:S(2)}) collective-permute-start(f32[32,640]{1,0:T(8,128)S(1)} %get-tuple-element.3), channel_id=1, source_target_pairs={{0,16},{4,20},{8,24},{12,28},{16,0},{20,4},{24,8},{28,12},{1,17},{... | collective-permute-start | bytes 245768 | tf_op jit(solution)/shard_map/ppermute | solution.py:25
  10.5 0.0 collective-permute-done.3
  10.5 1.9 %collective-permute-start = (f32[32,640]{1,0:T(8,128)S(1)}, f32[32,640]{1,0:T(8,128)S(1)}, u32[]{:S(2)}, u32[]{:S(2)}) collective-permute-start(f32[32,640]{1,0:T(8,128)S(1)} %get-tuple-element.3), channel_id=1, source_target_pairs={{0,24},{4,28},{8,16},{12,20},{16,8},{20,12},{24,0},{28,4},{1,25},{... | collective-permute-start | bytes 245768 | tf_op jit(solution)/shard_map/ppermute | solution.py:25
  12.4 1.1 %collective-permute-done.4 = f32[32,640]{1,0:T(8,128)S(1)} collective-permute-done((f32[32,640]{1,0:T(8,128)S(1)}, f32[32,640]{1,0:T(8,128)S(1)}, u32[]{:S(2)}, u32[]{:S(2)}) %collective-permute-start.4) | collective-permute-done | bytes 81952 | tf_op jit(solution)/shard_map/ppermute | solution.py:30
  13.5 0.0 collective-permute-done.5
  13.5 0.0 collective-permute-done.2
  13.5 0.7 %collective-permute-done.1 = f32[32,640]{1,0:T(8,128)S(1)} collective-permute-done((f32[32,640]{1,0:T(8,128)S(1)}, f32[32,640]{1,0:T(8,128)S(1)}, u32[]{:S(2)}, u32[]{:S(2)}) %collective-permute-start.1) | collective-permute-done | bytes 81952 | tf_op jit(solution)/shard_map/ppermute | solution.py:25
  14.3 1.5 %collective-permute-done = f32[32,640]{1,0:T(8,128)S(1)} collective-permute-done((f32[32,640]{1,0:T(8,128)S(1)}, f32[32,640]{1,0:T(8,128)S(1)}, u32[]{:S(2)}, u32[]{:S(2)}) %collective-permute-start) | collective-permute-done | bytes 81952 | tf_op jit(solution)/shard_map/ppermute | solution.py:25
  15.8 0.1 pad_maximum_fusion
  15.9 0.0 collective-permute-start.6
  16.0 0.1 multiply_reduce_fusion.1
  16.1 1.5 %collective-permute-done.6 = f32[128,640]{1,0:T(8,128)S(1)} collective-permute-done((f32[128,640]{1,0:T(8,128)S(1)}, f32[128,640]{1,0:T(8,128)S(1)}, u32[]{:S(2)}, u32[]{:S(2)}) %collective-permute-start.6) | collective-permute-done | bytes 327712 | tf_op jit(solution)/shard_map/ppermute | solution.py:34
  17.6 0.1 multiply_reduce_fusion
  17.7 0.1 fusion.22
  17.8 0.7 %fusion.2 = f32[128,256]{1,0:T(8,128)S(1)} fusion(f32[256,640]{1,0:T(8,128)S(1)} %constant_dynamic-update-slice_fusion, f32[128,640]{1,0:T(8,128)S(1)} %get-tuple-element.9, f32[256]{0:T(256)S(1)} %multiply_reduce_fusion, f32[128]{0:T(128)S(1)} %multiply_reduce_fusion.1), kind=kOutput, calls=%fused_computation.4 | convolution fusion | flops 201457664 | bytes 919040 | tf_op jit(solution)/shard_map/dot_general | solution.py:51
  18.5 0.3 fusion.20
  18.8 0.4 %fusion.23 = (f32[128]{0:T(128)S(1)}, f32[128,256]{1,0:T(8,128)S(1)}) fusion(f32[128,256]{1,0:T(8,128)S(1)} %fusion.2, f32[256,64]{1,0:T(8,128)S(1)} %get-tuple-element.5, f32[256,64]{1,0:T(8,128)S(1)} %get-tuple-element.4, f32[128,640]{1,0:T(8,128)S(1)} %get-tuple-element.9), kind=kOutput, calls=%fused_computation.44 | convolution fusion | flops 50429824 | bytes 590336 | tf_op jit(solution)/shard_map/dot_general | solution.py:57
  19.2 0.4 %convolution_subtract_fusion = f32[128,512]{1,0:T(8,128)S(1)} fusion(f32[128,256]{1,0:T(8,128)S(1)} %get-tuple-element.12, f32[256,640]{1,0:T(8,128)S(1)} %constant_dynamic-update-slice_fusion, f32[128,640]{1,0:T(8,128)S(1)} %get-tuple-element.9, f32[128]{0:T(128)S(1)} %get-tuple-element.11), kind=kOutput, calls=%fused_computation | convolution fusion | flops 201457664 | bytes 1180160 | tf_op jit(solution)/shard_map/dot_general | solution.py:62
  19.7 1.0 %collective-permute-start.9 = (f32[32,576]{1,0:T(8,128)S(1)}, f32[32,576]{1,0:T(8,128)S(1)}, u32[]{:S(2)}, u32[]{:S(2)}) collective-permute-start(f32[32,576]{1,0:T(8,128)S(1)} %get-tuple-element.7), channel_id=1, source_target_pairs={{8,0},{12,4},{0,8},{4,12},{24,16},{28,20},{16,24},{20,28},{9,1},{1... | collective-permute-start | bytes 221192 | tf_op jit(solution)/shard_map/ppermute | solution.py:25
  20.7 1.5 %collective-permute-start.8 = (f32[32,576]{1,0:T(8,128)S(1)}, f32[32,576]{1,0:T(8,128)S(1)}, u32[]{:S(2)}, u32[]{:S(2)}) collective-permute-start(f32[32,576]{1,0:T(8,128)S(1)} %get-tuple-element.8), channel_id=1, source_target_pairs={{16,0},{20,4},{24,8},{28,12},{0,16},{4,20},{8,24},{12,28},{17,1},{... | collective-permute-start | bytes 221192 | tf_op jit(solution)/shard_map/ppermute | solution.py:25
  22.2 1.0 %collective-permute-start.7 = (f32[32,576]{1,0:T(8,128)S(1)}, f32[32,576]{1,0:T(8,128)S(1)}, u32[]{:S(2)}, u32[]{:S(2)}) collective-permute-start(f32[32,576]{1,0:T(8,128)S(1)} %get-tuple-element.6), channel_id=1, source_target_pairs={{24,0},{28,4},{16,8},{20,12},{8,16},{12,20},{0,24},{4,28},{25,1},{... | collective-permute-start | bytes 221192 | tf_op jit(solution)/shard_map/ppermute | solution.py:25
  23.2 1.0 %collective-permute-done.9 = f32[32,576]{1,0:T(8,128)S(1)} collective-permute-done((f32[32,576]{1,0:T(8,128)S(1)}, f32[32,576]{1,0:T(8,128)S(1)}, u32[]{:S(2)}, u32[]{:S(2)}) %collective-permute-start.9) | collective-permute-done | bytes 73760 | tf_op jit(solution)/shard_map/ppermute | solution.py:25
  24.2 1.8 %collective-permute-done.8 = f32[32,576]{1,0:T(8,128)S(1)} collective-permute-done((f32[32,576]{1,0:T(8,128)S(1)}, f32[32,576]{1,0:T(8,128)S(1)}, u32[]{:S(2)}, u32[]{:S(2)}) %collective-permute-start.8) | collective-permute-done | bytes 73760 | tf_op jit(solution)/shard_map/ppermute | solution.py:25
  26.0 1.6 %collective-permute-done.7 = f32[32,576]{1,0:T(8,128)S(1)} collective-permute-done((f32[32,576]{1,0:T(8,128)S(1)}, f32[32,576]{1,0:T(8,128)S(1)}, u32[]{:S(2)}, u32[]{:S(2)}) %collective-permute-start.7) | collective-permute-done | bytes 73760 | tf_op jit(solution)/shard_map/ppermute | solution.py:25
  27.6 0.6 %slice.55 = f32[32,64]{1,0:T(8,128)} slice(f32[32,576]{1,0:T(8,128)S(1)} %fusion.16), slice={[0:32], [512:576]} | slice | bytes 16384 | tf_op jit(solution)/shard_map/slice | solution.py:68
  28.2 0.6 %slice.56 = f32[32,512]{1,0:T(8,128)} slice(f32[32,576]{1,0:T(8,128)S(1)} %fusion.16), slice={[0:32], [0:512]} | slice | bytes 131072 | tf_op jit(solution)/shard_map/slice | solution.py:68
  (10 shorter events, 0.1 us)
Async XLA Ops:
  0.6 0.9 %copy-start = (f32[32,64]{1,0:T(8,128)S(1)}, f32[32,64]{1,0:T(8,128)}, u32[]{:S(2)}) copy-start(f32[32,64]{1,0:T(8,128)} %param.7) | copy-start | bytes 24580
  0.6 0.9 %copy-start.1 = (f32[32,64]{1,0:T(8,128)S(1)}, f32[32,64]{1,0:T(8,128)}, u32[]{:S(2)}) copy-start(f32[32,64]{1,0:T(8,128)} %param.6) | copy-start | bytes 24580
  1.6 8.9 %collective-permute-start.3 = (f32[32,640]{1,0:T(8,128)S(1)}, f32[32,640]{1,0:T(8,128)S(1)}, u32[]{:S(2)}, u32[]{:S(2)}) collective-permute-start(f32[32,640]{1,0:T(8,128)S(1)} %get-tuple-element.3), channel_id=1, source_target_pairs={{0,3},{1,2},{2,1},{3,0},{4,7},{5,6},{6,5},{7,4},{8,11},{9,10},{10,... | collective-permute-start | bytes 245768 | tf_op jit(solution)/shard_map/ppermute | solution.py:30
  6.7 6.9 %collective-permute-start.4 = (f32[32,640]{1,0:T(8,128)S(1)}, f32[32,640]{1,0:T(8,128)S(1)}, u32[]{:S(2)}, u32[]{:S(2)}) collective-permute-start(f32[32,640]{1,0:T(8,128)S(1)} %get-tuple-element.3), channel_id=1, source_target_pairs={{0,2},{1,3},{2,0},{3,1},{4,6},{5,7},{6,4},{7,5},{8,10},{9,11},{10,... | collective-permute-start | bytes 245768 | tf_op jit(solution)/shard_map/ppermute | solution.py:30
  6.7 6.9 %collective-permute-start.5 = (f32[32,640]{1,0:T(8,128)S(1)}, f32[32,640]{1,0:T(8,128)S(1)}, u32[]{:S(2)}, u32[]{:S(2)}) collective-permute-start(f32[32,640]{1,0:T(8,128)S(1)} %get-tuple-element.3), channel_id=1, source_target_pairs={{0,1},{1,0},{2,3},{3,2},{4,5},{5,4},{6,7},{7,6},{8,9},{9,8},{10,11... | collective-permute-start | bytes 245768 | tf_op jit(solution)/shard_map/ppermute | solution.py:30
  7.3 6.2 %collective-permute-start.2 = (f32[32,640]{1,0:T(8,128)S(1)}, f32[32,640]{1,0:T(8,128)S(1)}, u32[]{:S(2)}, u32[]{:S(2)}) collective-permute-start(f32[32,640]{1,0:T(8,128)S(1)} %get-tuple-element.3), channel_id=1, source_target_pairs={{0,8},{4,12},{8,0},{12,4},{16,24},{20,28},{24,16},{28,20},{1,9},{5... | collective-permute-start | bytes 245768 | tf_op jit(solution)/shard_map/ppermute | solution.py:25
  9.0 5.3 %collective-permute-start.1 = (f32[32,640]{1,0:T(8,128)S(1)}, f32[32,640]{1,0:T(8,128)S(1)}, u32[]{:S(2)}, u32[]{:S(2)}) collective-permute-start(f32[32,640]{1,0:T(8,128)S(1)} %get-tuple-element.3), channel_id=1, source_target_pairs={{0,16},{4,20},{8,24},{12,28},{16,0},{20,4},{24,8},{28,12},{1,17},{... | collective-permute-start | bytes 245768 | tf_op jit(solution)/shard_map/ppermute | solution.py:25
  10.5 5.3 %collective-permute-start = (f32[32,640]{1,0:T(8,128)S(1)}, f32[32,640]{1,0:T(8,128)S(1)}, u32[]{:S(2)}, u32[]{:S(2)}) collective-permute-start(f32[32,640]{1,0:T(8,128)S(1)} %get-tuple-element.3), channel_id=1, source_target_pairs={{0,24},{4,28},{8,16},{12,20},{16,8},{20,12},{24,0},{28,4},{1,25},{... | collective-permute-start | bytes 245768 | tf_op jit(solution)/shard_map/ppermute | solution.py:25
  15.9 1.7 %collective-permute-start.6 = (f32[128,640]{1,0:T(8,128)S(1)}, f32[128,640]{1,0:T(8,128)S(1)}, u32[]{:S(2)}, u32[]{:S(2)}) collective-permute-start(f32[128,640]{1,0:T(8,128)S(1)} %get-tuple-element.10), channel_id=1, source_target_pairs={{0,4},{4,0},{8,12},{12,8},{16,20},{20,16},{24,28},{28,24},{1,5},{5... | collective-permute-start | bytes 983048 | tf_op jit(solution)/shard_map/ppermute | solution.py:34
  19.7 4.6 %collective-permute-start.9 = (f32[32,576]{1,0:T(8,128)S(1)}, f32[32,576]{1,0:T(8,128)S(1)}, u32[]{:S(2)}, u32[]{:S(2)}) collective-permute-start(f32[32,576]{1,0:T(8,128)S(1)} %get-tuple-element.7), channel_id=1, source_target_pairs={{8,0},{12,4},{0,8},{4,12},{24,16},{28,20},{16,24},{20,28},{9,1},{1... | collective-permute-start | bytes 221192 | tf_op jit(solution)/shard_map/ppermute | solution.py:25
  20.7 5.3 %collective-permute-start.8 = (f32[32,576]{1,0:T(8,128)S(1)}, f32[32,576]{1,0:T(8,128)S(1)}, u32[]{:S(2)}, u32[]{:S(2)}) collective-permute-start(f32[32,576]{1,0:T(8,128)S(1)} %get-tuple-element.8), channel_id=1, source_target_pairs={{16,0},{20,4},{24,8},{28,12},{0,16},{4,20},{8,24},{12,28},{17,1},{... | collective-permute-start | bytes 221192 | tf_op jit(solution)/shard_map/ppermute | solution.py:25
  22.2 5.3 %collective-permute-start.7 = (f32[32,576]{1,0:T(8,128)S(1)}, f32[32,576]{1,0:T(8,128)S(1)}, u32[]{:S(2)}, u32[]{:S(2)}) collective-permute-start(f32[32,576]{1,0:T(8,128)S(1)} %get-tuple-element.6), channel_id=1, source_target_pairs={{24,0},{28,4},{16,8},{20,12},{8,16},{12,20},{0,24},{4,28},{25,1},{... | collective-permute-start | bytes 221192 | tf_op jit(solution)/shard_map/ppermute | solution.py:25

commit v2 on v1

v2 whole, which is shorter than its diff:
```python
import functools

import jax
import jax.numpy as jnp
from jax import lax
from jax.experimental import pallas as pl
from jax.experimental.pallas import tpu as pltpu
from jax.sharding import PartitionSpec as P

HIGH = lax.Precision.HIGHEST
ROWS_RULE = (((1,), (1,)), ((), ()))
PLAIN_RULE = (((1,), (0,)), ((), ()))
CORES = 2
MIB = 2**20


def whole(count):
    return [pl.BlockSpec(memory_space=pltpu.VMEM)] * count


def dot(left, right, rule=PLAIN_RULE):
    return lax.dot_general(left, right, rule, precision=HIGH, preferred_element_type=jnp.float32)


def partner(position, step, length):
    if length & (length - 1) == 0:
        return position ^ step
    return (position + step) % length


def over_plane(value, step, back=False):
    blocks = lax.axis_size("blk")
    places = blocks // CORES
    pairs = [
        (p * CORES + c, partner(p, step, places) * CORES + c)
        for p in range(places)
        for c in range(CORES)
    ]
    return lax.ppermute(value, "blk", [(b, a) for a, b in pairs] if back else pairs)


def over_line(value, step):
    length = lax.axis_size("sub")
    return lax.ppermute(value, "sub", [(p, partner(p, step, length)) for p in range(length)])


def over_cores(value):
    return lax.ppermute(value, "blk", [(i, i ^ 1) for i in range(lax.axis_size("blk"))])


def gathered_line(value):
    length = lax.axis_size("sub")
    if length & (length - 1):
        return [value] + [over_line(value, step) for step in range(length - 1, 0, -1)]
    pieces, step = [value], length // 2
    while step:
        pieces = pieces + [over_line(piece, step) for piece in pieces]
        step //= 2
    return pieces


def stage_body(row_count, column_count, adds, width, *refs):
    columns_end = row_count + column_count
    sums, outs = refs[columns_end : columns_end + row_count * adds], refs[-row_count:]
    rows = jnp.concatenate([ref[...] for ref in refs[:row_count]], axis=0)
    columns = jnp.concatenate([ref[...] for ref in refs[row_count:columns_end]], axis=0)
    probes = (rows.shape[1] - width) // 2
    row_scaled, column_scaled = rows[:, :width], columns[:, :width]
    row_norms = jnp.sum(row_scaled * row_scaled, axis=1, keepdims=True)
    ones = jnp.ones((8, width), jnp.float32)
    column_norms = dot(ones, column_scaled * column_scaled, ROWS_RULE)[:1]
    inner = dot(row_scaled, column_scaled, ROWS_RULE)
    kernel = jnp.exp(-0.5 * (row_norms + column_norms - 2.0 * inner))
    column_probes = columns[:, width : width + probes]
    swapped = jnp.concatenate([columns[:, width + probes :], column_probes], axis=1)
    weight = kernel * dot(rows[:, width:], swapped, ROWS_RULE)
    product = dot(kernel, column_probes)
    gradient = dot(weight, column_scaled) - jnp.sum(weight, axis=1, keepdims=True) * row_scaled
    points = outs[0].shape[0]
    for place, out in enumerate(outs):
        part = slice(place * points, (place + 1) * points)
        if adds:
            out[:, :width] = sums[place][:, :width] + gradient[part]
            out[:, width:] = sums[place][:, width:] + product[part]
        else:
            out[:, :width] = gradient[part]
            out[:, width:] = product[part]


def stage(rows, columns, sums, width):
    points, full = rows[0].shape
    probes = (full - width) // 2
    m, n = points * len(rows), points * len(columns)
    operands = [*rows, *columns, *(sums or ())]
    flops = 12 * m * n * (2 * width + 3 * probes)
    held = 4 * (6 * (m + n) * full + 8 * m * n)
    return pl.pallas_call(
        functools.partial(stage_body, len(rows), len(columns), bool(sums), width),
        out_shape=[jax.ShapeDtypeStruct((points, width + probes), jnp.float32)] * len(rows),
        in_specs=whole(len(operands)),
        out_specs=whole(len(rows)),
        compiler_params=pltpu.CompilerParams(vmem_limit_bytes=max(4 * MIB, held)),
        cost_estimate=pl.CostEstimate(
            flops=flops, bytes_accessed=4 * (m + n) * full, transcendentals=m * n
        ),
    )(*operands)


def total_body(*refs):
    parts, (product, gradient) = refs[:-2], refs[-2:]
    total = parts[0][...]
    for part in parts[1:]:
        total = total + part[...]
    gradient[...] = total[:, : gradient.shape[1]]
    product[...] = total[:, gradient.shape[1] :]


def total(parts, width):
    points, full = parts[0].shape
    return pl.pallas_call(
        total_body,
        out_shape=(
            jax.ShapeDtypeStruct((points, full - width), jnp.float32),
            jax.ShapeDtypeStruct((points, width), jnp.float32),
        ),
        in_specs=whole(len(parts)),
        out_specs=tuple(whole(2)),
        compiler_params=pltpu.CompilerParams(vmem_limit_bytes=4 * MIB),
    )(*parts)


def on_device(features, lengthscale, probes, cotangent):
    width = features.shape[1]
    places = lax.axis_size("blk") // CORES
    scaled = features / lengthscale[None, :]
    data = jnp.concatenate([scaled, probes, cotangent], axis=1)
    *early, late = gathered_line(data)
    rows = [data] + [over_plane(data, step) for step in range(places - 1, 0, -1)]
    sums = stage(rows, early + [over_cores(piece) for piece in early], None, width)
    sums = stage(rows, [late, over_cores(late)], sums, width)
    back = [over_plane(sums[places - step], step, True) for step in range(places - 1, 0, -1)]
    return total([sums[0]] + back, width)


def solution(mesh):
    spec = P(("blk", "sub"), None)
    return jax.shard_map(
        on_device, mesh=mesh, in_specs=(spec, P(), spec, spec), out_specs=(spec, spec), check_vma=False
    )
```

time: 29.3 us -> 25.8 us (0.88); the launches traced: 28.8 us -> 25.7 us
  Pallas kernels: 0 us -> 3.02 us
  waiting for transfers between devices: 9.21 us -> 6.96 us
  matrix products: 1.81 us -> 0 us
  local copies, waits for them, and re-layouts: 1.39 us -> 0.01 us
  starting transfers between devices: 14.4 us -> 14 us
  other arithmetic: 1.28 us -> 0.94 us
    pallas_call x0 -> x3, Pallas kernels: none -> 3.02 us  [the longest x2 2.37 us: stage(): pl.pallas_call(functools.partial(stage_body, len(rows), len(columns), boo...]
    dot_general x4 -> x0, matrix products: 1.81 us -> none  [the longest x1 0.68 us: on_device(): lax.dot_general(row_scaled, column_scaled, ROWS_RULE, precision=HIGH, pre...]
    slice x3 -> x0, local copies, waits for them, and re-layouts: 1.33 us -> none  [the longest x2 1.24 us: on_device(): return (total[:, width:], total[:, :width])]
    ppermute x1 -> x4, waiting for transfers between devices: 1.46 us -> 0.32 us  [over_cores(): lax.ppermute(value, 'blk', [(i, i ^ 1) for i in range(lax.axis_size('blk'...]
    ppermute x6, starting transfers between devices: 8.65 us -> 7.96 us  [over_plane(): lax.ppermute(value, 'blk', [(b, a) for a, b in pairs] if back else pairs)]
    ppermute x3, waiting for transfers between devices: 1.13 us -> 0.51 us  [over_line(): lax.ppermute(value, 'sub', [(p, partner(p, step, length)) for p in range(...]
    ppermute x6, waiting for transfers between devices: 6.63 us -> 6.13 us  [over_plane(): lax.ppermute(value, 'blk', [(b, a) for a, b in pairs] if back else pairs)]
    ppermute x3, starting transfers between devices: 5.7 us -> 6.07 us  [over_line(): lax.ppermute(value, 'sub', [(p, partner(p, step, length)) for p in range(...]
  transfers between devices with their start and end apart: 10 -> 13, of which waited for: 7 -> 7; matrix products, arithmetic and copies ran while one was open for 0% -> 0% of each run, Pallas kernels for 0% -> 5%
where the time goes in v2:
time: 25.8 us; the launch traced here: 25.7 us
  starting transfers between devices  14 us (54%)
  waiting for transfers between devices  6.96 us (27%)
  Pallas kernels  3.02 us (12%)
  other arithmetic  0.94 us (4%)
  between operations  0.7 us (3%)
    ppermute x6, starting transfers between devices, over_plane(): lax.ppermute(value, 'blk', [(b, a) for a, b in pairs] if back else pairs)  7.96 us
    ppermute x6, waiting for transfers between devices, over_plane(): lax.ppermute(value, 'blk', [(b, a) for a, b in pairs] if back else pairs)  6.13 us
    ppermute x3, starting transfers between devices, over_line(): lax.ppermute(value, 'sub', [(p, partner(p, step, length)) for p in range(...  6.07 us
    pallas_call x2, Pallas kernels, stage(): pl.pallas_call(functools.partial(stage_body, len(rows), len(columns), boo...  2.37 us
    div x1, other arithmetic, on_device(): scaled = features / lengthscale[None, :]  0.86 us
    pallas_call x1, Pallas kernels, total(): pl.pallas_call(total_body, out_shape=(jax.ShapeDtypeStruct((points, full...  0.65 us
  transfers between devices with their start and end apart: 13, of which 7 were waited for; matrix products, arithmetic and copies ran while one was open for 0% of the time, Pallas kernels for 5%

profile of v2, /device:TPU:0, one launch (start us, length us, event | category | flops | bytes accessed | tf_op | source)
XLA Modules:
  0.0 25.7 jit_solution(1165116705234953190)
XLA Ops:
  0.6 0.0 copy-start.1
  0.7 0.9 %broadcast_divide_fusion = f32[32,512]{1,0:T(8,128)S(1)} fusion(f32[32,512]{1,0:T(8,128)} %param.4, f32[512]{0:T(512)} %param.5), kind=kLoop, calls=%fused_computation.1 | loop fusion | flops 16384 | bytes 133120 | tf_op jit(solution)/shard_map/div | solution.py:135
  1.5 0.1 pad_maximum_fusion.refs_0_.refs_4_
  1.6 4.0 %collective-permute-start.3 = (f32[32,640]{1,0:T(8,128)S(1)}, f32[32,640]{1,0:T(8,128)S(1)}, u32[]{:S(2)}, u32[]{:S(2)}) collective-permute-start(f32[32,640]{1,0:T(8,128)S(1)} %pad_maximum_fusion.refs_0_.refs_4_), channel_id=1, source_target_pairs={{0,2},{1,3},{2,0},{3,1},{4,6},{5,7},{6,4},{7,5},{8,10},{9,11},{10,... | collective-permute-start | bytes 245768 | tf_op jit(solution)/shard_map/ppermute | solution.py:44
  5.7 1.6 %collective-permute-start.6 = (f32[32,640]{1,0:T(8,128)S(1)}, f32[32,640]{1,0:T(8,128)S(1)}, u32[]{:S(2)}, u32[]{:S(2)}) collective-permute-start(f32[32,640]{1,0:T(8,128)S(1)} %pad_maximum_fusion.refs_0_.refs_4_), channel_id=1, source_target_pairs={{0,1},{1,0},{2,3},{3,2},{4,5},{5,4},{6,7},{7,6},{8,9},{9,8},{10,11... | collective-permute-start | bytes 245768 | tf_op jit(solution)/shard_map/ppermute | solution.py:44
  7.2 2.4 %collective-permute-start = (f32[32,640]{1,0:T(8,128)S(1)}, f32[32,640]{1,0:T(8,128)S(1)}, u32[]{:S(2)}, u32[]{:S(2)}) collective-permute-start(f32[32,640]{1,0:T(8,128)S(1)} %pad_maximum_fusion.refs_0_.refs_4_), channel_id=1, source_target_pairs={{0,24},{4,28},{8,16},{12,20},{16,8},{20,12},{24,0},{28,4},{1,25},{... | collective-permute-start | bytes 245768 | tf_op jit(solution)/shard_map/ppermute | solution.py:39
  9.7 0.5 %collective-permute-start.1 = (f32[32,640]{1,0:T(8,128)S(1)}, f32[32,640]{1,0:T(8,128)S(1)}, u32[]{:S(2)}, u32[]{:S(2)}) collective-permute-start(f32[32,640]{1,0:T(8,128)S(1)} %pad_maximum_fusion.refs_0_.refs_4_), channel_id=1, source_target_pairs={{0,16},{4,20},{8,24},{12,28},{16,0},{20,4},{24,8},{28,12},{1,17},{... | collective-permute-start | bytes 245768 | tf_op jit(solution)/shard_map/ppermute | solution.py:39
  10.2 0.0 collective-permute-done.3.refs_5_
  10.2 0.5 %collective-permute-start.4 = (f32[32,640]{1,0:T(8,128)S(1)}, f32[32,640]{1,0:T(8,128)S(1)}, u32[]{:S(2)}, u32[]{:S(2)}) collective-permute-start(f32[32,640]{1,0:T(8,128)S(1)} %collective-permute-done.3.refs_5_), channel_id=1, source_target_pairs={{0,1},{1,0},{2,3},{3,2},{4,5},{5,4},{6,7},{7,6},{8,9},{9,8},{10,11... | collective-permute-start | bytes 245768 | tf_op jit(solution)/shard_map/ppermute | solution.py:44
  10.6 1.5 %collective-permute-start.2 = (f32[32,640]{1,0:T(8,128)S(1)}, f32[32,640]{1,0:T(8,128)S(1)}, u32[]{:S(2)}, u32[]{:S(2)}) collective-permute-start(f32[32,640]{1,0:T(8,128)S(1)} %pad_maximum_fusion.refs_0_.refs_4_), channel_id=1, source_target_pairs={{0,8},{4,12},{8,0},{12,4},{16,24},{20,28},{24,16},{28,20},{1,9},{5... | collective-permute-start | bytes 245768 | tf_op jit(solution)/shard_map/ppermute | solution.py:39
  12.1 0.0 collective-permute-done.6.refs_6_
  12.1 0.0 collective-permute-start.7
  12.1 0.6 %collective-permute-done.refs_1_ = f32[32,640]{1,0:T(8,128)S(1)} collective-permute-done((f32[32,640]{1,0:T(8,128)S(1)}, f32[32,640]{1,0:T(8,128)S(1)}, u32[]{:S(2)}, u32[]{:S(2)}) %collective-permute-start) | collective-permute-done | bytes 81952 | tf_op jit(solution)/shard_map/ppermute | solution.py:39
  12.7 0.0 collective-permute-start.8
  12.7 1.4 %collective-permute-done.1.refs_2_ = f32[32,640]{1,0:T(8,128)S(1)} collective-permute-done((f32[32,640]{1,0:T(8,128)S(1)}, f32[32,640]{1,0:T(8,128)S(1)}, u32[]{:S(2)}, u32[]{:S(2)}) %collective-permute-start.1) | collective-permute-done | bytes 81952 | tf_op jit(solution)/shard_map/ppermute | solution.py:39
  14.1 0.0 collective-permute-start.9
  14.1 0.5 %collective-permute-done.4.refs_4_ = f32[32,640]{1,0:T(8,128)S(1)} collective-permute-done((f32[32,640]{1,0:T(8,128)S(1)}, f32[32,640]{1,0:T(8,128)S(1)}, u32[]{:S(2)}, u32[]{:S(2)}) %collective-permute-start.4) | collective-permute-done | bytes 81952 | tf_op jit(solution)/shard_map/ppermute | solution.py:44
  14.6 0.0 collective-permute-start.5
  14.6 0.4 %collective-permute-done.2.refs_3_ = f32[32,640]{1,0:T(8,128)S(1)} collective-permute-done((f32[32,640]{1,0:T(8,128)S(1)}, f32[32,640]{1,0:T(8,128)S(1)}, u32[]{:S(2)}, u32[]{:S(2)}) %collective-permute-start.2) | collective-permute-done | bytes 81952 | tf_op jit(solution)/shard_map/ppermute | solution.py:39
  15.1 0.0 collective-permute-done.7.refs_7_
  15.1 0.0 collective-permute-done.8.refs_8_
  15.1 0.3 %collective-permute-done.9.refs_9_ = f32[32,640]{1,0:T(8,128)S(1)} collective-permute-done((f32[32,640]{1,0:T(8,128)S(1)}, f32[32,640]{1,0:T(8,128)S(1)}, u32[]{:S(2)}, u32[]{:S(2)}) %collective-permute-start.9) | collective-permute-done | bytes 81952 | tf_op jit(solution)/shard_map/ppermute | solution.py:48
  15.4 1.4 %shard_map.59 = (f32[32,576]{1,0:T(8,128)S(1)}, f32[32,576]{1,0:T(8,128)S(1)}, f32[32,576]{1,0:T(8,128)S(1)}, f32[32,576]{1,0:T(8,128)S(1)}) custom-call(f32[32,640]{1,0:T(8,128)S(1)} %pad_maximum_fusion.refs_0_.refs_4_, f32[32,640]{1,0:T(8,128)S(1)} %collective-permute-done.refs_1_, f32[32,640]{1,0:T(8,128)S(1)} %collective-permute-done.1.refs_2_, ...), custom_call_target="tpu_custom_call" | custom-call | flops 358612992 | bytes 819200 | tf_op jit(solution)/shard_map/pallas_call | solution.py:97
  16.8 0.0 collective-permute-done.5.refs_5_
  16.8 1.0 %shard_map.60 = (f32[32,576]{1,0:T(8,128)S(1)}, f32[32,576]{1,0:T(8,128)S(1)}, f32[32,576]{1,0:T(8,128)S(1)}, f32[32,576]{1,0:T(8,128)S(1)}) custom-call(f32[32,640]{1,0:T(8,128)S(1)} %pad_maximum_fusion.refs_0_.refs_4_, f32[32,640]{1,0:T(8,128)S(1)} %collective-permute-done.refs_1_, f32[32,640]{1,0:T(8,128)S(1)} %collective-permute-done.1.refs_2_, ...), custom_call_target="tpu_custom_call" | custom-call | flops 119537664 | bytes 491520 | tf_op jit(solution)/shard_map/pallas_call | solution.py:97
  17.8 2.2 %collective-permute-start.10 = (f32[32,576]{1,0:T(8,128)S(1)}, f32[32,576]{1,0:T(8,128)S(1)}, u32[]{:S(2)}, u32[]{:S(2)}) collective-permute-start(f32[32,576]{1,0:T(8,128)S(1)} %get-tuple-element.15), channel_id=1, source_target_pairs={{24,0},{28,4},{16,8},{20,12},{8,16},{12,20},{0,24},{4,28},{25,1},{... | collective-permute-start | bytes 221192 | tf_op jit(solution)/shard_map/ppermute | solution.py:39
  20.0 0.5 %collective-permute-start.11 = (f32[32,576]{1,0:T(8,128)S(1)}, f32[32,576]{1,0:T(8,128)S(1)}, u32[]{:S(2)}, u32[]{:S(2)}) collective-permute-start(f32[32,576]{1,0:T(8,128)S(1)} %get-tuple-element.16), channel_id=1, source_target_pairs={{16,0},{20,4},{24,8},{28,12},{0,16},{4,20},{8,24},{12,28},{17,1},{... | collective-permute-start | bytes 221192 | tf_op jit(solution)/shard_map/ppermute | solution.py:39
  20.5 0.9 %collective-permute-start.12 = (f32[32,576]{1,0:T(8,128)S(1)}, f32[32,576]{1,0:T(8,128)S(1)}, u32[]{:S(2)}, u32[]{:S(2)}) collective-permute-start(f32[32,576]{1,0:T(8,128)S(1)} %get-tuple-element.17), channel_id=1, source_target_pairs={{8,0},{12,4},{0,8},{4,12},{24,16},{28,20},{16,24},{20,28},{9,1},{1... | collective-permute-start | bytes 221192 | tf_op jit(solution)/shard_map/ppermute | solution.py:39
  21.4 2.1 %collective-permute-done.10.refs_1_ = f32[32,576]{1,0:T(8,128)S(1)} collective-permute-done((f32[32,576]{1,0:T(8,128)S(1)}, f32[32,576]{1,0:T(8,128)S(1)}, u32[]{:S(2)}, u32[]{:S(2)}) %collective-permute-start.10) | collective-permute-done | bytes 73760 | tf_op jit(solution)/shard_map/ppermute | solution.py:39
  23.4 1.6 %collective-permute-done.11.refs_2_ = f32[32,576]{1,0:T(8,128)S(1)} collective-permute-done((f32[32,576]{1,0:T(8,128)S(1)}, f32[32,576]{1,0:T(8,128)S(1)}, u32[]{:S(2)}, u32[]{:S(2)}) %collective-permute-start.11) | collective-permute-done | bytes 73760 | tf_op jit(solution)/shard_map/ppermute | solution.py:39
  25.0 0.0 collective-permute-done.12.refs_3_
  25.0 0.6 %shard_map.61 = (f32[32,64]{1,0:T(8,128)}, f32[32,512]{1,0:T(8,128)}) custom-call(f32[32,576]{1,0:T(8,128)S(1)} %get-tuple-element.14.refs_0_, f32[32,576]{1,0:T(8,128)S(1)} %collective-permute-done.10.refs_1_, f32[32,576]{1,0:T(8,128)S(1)} %collective-permute-done.11.refs_2_, f32[32,576]{1,0:T(8,128)S(1)} %collective-permute-done.12.refs_3_), custom_call_target="tpu_custom_call" | custom-call | tf_op jit(solution)/shard_map/pallas_call | solution.py:120
  (3 shorter events, 0.0 us)
Async XLA Ops:
  0.6 0.9 %copy-start.1 = (f32[32,64]{1,0:T(8,128)S(1)}, f32[32,64]{1,0:T(8,128)}, u32[]{:S(2)}) copy-start(f32[32,64]{1,0:T(8,128)} %param.6) | copy-start | bytes 24580
  0.6 0.9 %copy-start = (f32[32,64]{1,0:T(8,128)S(1)}, f32[32,64]{1,0:T(8,128)}, u32[]{:S(2)}) copy-start(f32[32,64]{1,0:T(8,128)} %param.7) | copy-start | bytes 24580
  1.6 8.6 %collective-permute-start.3 = (f32[32,640]{1,0:T(8,128)S(1)}, f32[32,640]{1,0:T(8,128)S(1)}, u32[]{:S(2)}, u32[]{:S(2)}) collective-permute-start(f32[32,640]{1,0:T(8,128)S(1)} %pad_maximum_fusion.refs_0_.refs_4_), channel_id=1, source_target_pairs={{0,2},{1,3},{2,0},{3,1},{4,6},{5,7},{6,4},{7,5},{8,10},{9,11},{10,... | collective-permute-start | bytes 245768 | tf_op jit(solution)/shard_map/ppermute | solution.py:44
  5.7 6.4 %collective-permute-start.6 = (f32[32,640]{1,0:T(8,128)S(1)}, f32[32,640]{1,0:T(8,128)S(1)}, u32[]{:S(2)}, u32[]{:S(2)}) collective-permute-start(f32[32,640]{1,0:T(8,128)S(1)} %pad_maximum_fusion.refs_0_.refs_4_), channel_id=1, source_target_pairs={{0,1},{1,0},{2,3},{3,2},{4,5},{5,4},{6,7},{7,6},{8,9},{9,8},{10,11... | collective-permute-start | bytes 245768 | tf_op jit(solution)/shard_map/ppermute | solution.py:44
  7.2 5.4 %collective-permute-start = (f32[32,640]{1,0:T(8,128)S(1)}, f32[32,640]{1,0:T(8,128)S(1)}, u32[]{:S(2)}, u32[]{:S(2)}) collective-permute-start(f32[32,640]{1,0:T(8,128)S(1)} %pad_maximum_fusion.refs_0_.refs_4_), channel_id=1, source_target_pairs={{0,24},{4,28},{8,16},{12,20},{16,8},{20,12},{24,0},{28,4},{1,25},{... | collective-permute-start | bytes 245768 | tf_op jit(solution)/shard_map/ppermute | solution.py:39
  9.7 4.4 %collective-permute-start.1 = (f32[32,640]{1,0:T(8,128)S(1)}, f32[32,640]{1,0:T(8,128)S(1)}, u32[]{:S(2)}, u32[]{:S(2)}) collective-permute-start(f32[32,640]{1,0:T(8,128)S(1)} %pad_maximum_fusion.refs_0_.refs_4_), channel_id=1, source_target_pairs={{0,16},{4,20},{8,24},{12,28},{16,0},{20,4},{24,8},{28,12},{1,17},{... | collective-permute-start | bytes 245768 | tf_op jit(solution)/shard_map/ppermute | solution.py:39
  10.2 4.4 %collective-permute-start.4 = (f32[32,640]{1,0:T(8,128)S(1)}, f32[32,640]{1,0:T(8,128)S(1)}, u32[]{:S(2)}, u32[]{:S(2)}) collective-permute-start(f32[32,640]{1,0:T(8,128)S(1)} %collective-permute-done.3.refs_5_), channel_id=1, source_target_pairs={{0,1},{1,0},{2,3},{3,2},{4,5},{5,4},{6,7},{7,6},{8,9},{9,8},{10,11... | collective-permute-start | bytes 245768 | tf_op jit(solution)/shard_map/ppermute | solution.py:44
  10.6 4.4 %collective-permute-start.2 = (f32[32,640]{1,0:T(8,128)S(1)}, f32[32,640]{1,0:T(8,128)S(1)}, u32[]{:S(2)}, u32[]{:S(2)}) collective-permute-start(f32[32,640]{1,0:T(8,128)S(1)} %pad_maximum_fusion.refs_0_.refs_4_), channel_id=1, source_target_pairs={{0,8},{4,12},{8,0},{12,4},{16,24},{20,28},{24,16},{28,20},{1,9},{5... | collective-permute-start | bytes 245768 | tf_op jit(solution)/shard_map/ppermute | solution.py:39
  12.1 3.0 %collective-permute-start.7 = (f32[32,640]{1,0:T(8,128)S(1)}, f32[32,640]{1,0:T(8,128)S(1)}, u32[]{:S(2)}, u32[]{:S(2)}) collective-permute-start(f32[32,640]{1,0:T(8,128)S(1)} %pad_maximum_fusion.refs_0_.refs_4_), channel_id=1, source_target_pairs={{0,4},{4,0},{8,12},{12,8},{16,20},{20,16},{24,28},{28,24},{1,5},{5... | collective-permute-start | bytes 245768 | tf_op jit(solution)/shard_map/ppermute | solution.py:48
  12.7 2.4 %collective-permute-start.8 = (f32[32,640]{1,0:T(8,128)S(1)}, f32[32,640]{1,0:T(8,128)S(1)}, u32[]{:S(2)}, u32[]{:S(2)}) collective-permute-start(f32[32,640]{1,0:T(8,128)S(1)} %collective-permute-done.3.refs_5_), channel_id=1, source_target_pairs={{0,4},{4,0},{8,12},{12,8},{16,20},{20,16},{24,28},{28,24},{1,5},{5... | collective-permute-start | bytes 245768 | tf_op jit(solution)/shard_map/ppermute | solution.py:48
  14.1 1.3 %collective-permute-start.9 = (f32[32,640]{1,0:T(8,128)S(1)}, f32[32,640]{1,0:T(8,128)S(1)}, u32[]{:S(2)}, u32[]{:S(2)}) collective-permute-start(f32[32,640]{1,0:T(8,128)S(1)} %collective-permute-done.6.refs_6_), channel_id=1, source_target_pairs={{0,4},{4,0},{8,12},{12,8},{16,20},{20,16},{24,28},{28,24},{1,5},{5... | collective-permute-start | bytes 245768 | tf_op jit(solution)/shard_map/ppermute | solution.py:48
  14.6 2.2 %collective-permute-start.5 = (f32[32,640]{1,0:T(8,128)S(1)}, f32[32,640]{1,0:T(8,128)S(1)}, u32[]{:S(2)}, u32[]{:S(2)}) collective-permute-start(f32[32,640]{1,0:T(8,128)S(1)} %collective-permute-done.4.refs_4_), channel_id=1, source_target_pairs={{0,4},{4,0},{8,12},{12,8},{16,20},{20,16},{24,28},{28,24},{1,5},{5... | collective-permute-start | bytes 245768 | tf_op jit(solution)/shard_map/ppermute | solution.py:48
  17.8 5.6 %collective-permute-start.10 = (f32[32,576]{1,0:T(8,128)S(1)}, f32[32,576]{1,0:T(8,128)S(1)}, u32[]{:S(2)}, u32[]{:S(2)}) collective-permute-start(f32[32,576]{1,0:T(8,128)S(1)} %get-tuple-element.15), channel_id=1, source_target_pairs={{24,0},{28,4},{16,8},{20,12},{8,16},{12,20},{0,24},{4,28},{25,1},{... | collective-permute-start | bytes 221192 | tf_op jit(solution)/shard_map/ppermute | solution.py:39
  20.0 5.0 %collective-permute-start.11 = (f32[32,576]{1,0:T(8,128)S(1)}, f32[32,576]{1,0:T(8,128)S(1)}, u32[]{:S(2)}, u32[]{:S(2)}) collective-permute-start(f32[32,576]{1,0:T(8,128)S(1)} %get-tuple-element.16), channel_id=1, source_target_pairs={{16,0},{20,4},{24,8},{28,12},{0,16},{4,20},{8,24},{12,28},{17,1},{... | collective-permute-start | bytes 221192 | tf_op jit(solution)/shard_map/ppermute | solution.py:39
  20.5 4.5 %collective-permute-start.12 = (f32[32,576]{1,0:T(8,128)S(1)}, f32[32,576]{1,0:T(8,128)S(1)}, u32[]{:S(2)}, u32[]{:S(2)}) collective-permute-start(f32[32,576]{1,0:T(8,128)S(1)} %get-tuple-element.17), channel_id=1, source_target_pairs={{8,0},{12,4},{0,8},{4,12},{24,16},{28,20},{16,24},{20,28},{9,1},{1... | collective-permute-start | bytes 221192 | tf_op jit(solution)/shard_map/ppermute | solution.py:39

commit v3 on v2

--- a/solution.py
+++ b/solution.py
@@ -11,6 +11,7 @@
 ROWS_RULE = (((1,), (1,)), ((), ()))
 PLAIN_RULE = (((1,), (0,)), ((), ()))
 CORES = 2
+LANES = 128
 MIB = 2**20
 
 
@@ -67,8 +68,8 @@
     probes = (rows.shape[1] - width) // 2
     row_scaled, column_scaled = rows[:, :width], columns[:, :width]
     row_norms = jnp.sum(row_scaled * row_scaled, axis=1, keepdims=True)
-    ones = jnp.ones((8, width), jnp.float32)
-    column_norms = dot(ones, column_scaled * column_scaled, ROWS_RULE)[:1]
+    column_norms = jnp.sum(column_scaled * column_scaled, axis=1, keepdims=True)
+    column_norms = jnp.broadcast_to(column_norms, (column_norms.shape[0], LANES)).T[:1]
     inner = dot(row_scaled, column_scaled, ROWS_RULE)
     kernel = jnp.exp(-0.5 * (row_norms + column_norms - 2.0 * inner))
     column_probes = columns[:, width : width + probes]

time: 25.8 us -> 25.6 us (level)
  no operation moved by 1% of the time
where the time goes in v3:
time: 25.6 us; the launch traced here: 25.5 us
  starting transfers between devices  14 us (55%)
  waiting for transfers between devices  6.96 us (27%)
  Pallas kernels  2.8 us (11%)
  other arithmetic  0.94 us (4%)
  between operations  0.7 us (3%)
    ppermute x6, starting transfers between devices, over_plane(): lax.ppermute(value, 'blk', [(b, a) for a, b in pairs] if back else pairs)  7.96 us
    ppermute x6, waiting for transfers between devices, over_plane(): lax.ppermute(value, 'blk', [(b, a) for a, b in pairs] if back else pairs)  6.13 us
    ppermute x3, starting transfers between devices, over_line(): lax.ppermute(value, 'sub', [(p, partner(p, step, length)) for p in range(...  6.07 us
    pallas_call x2, Pallas kernels, stage(): pl.pallas_call(functools.partial(stage_body, len(rows), len(columns), boo...  2.15 us
    div x1, other arithmetic, on_device(): scaled = features / lengthscale[None, :]  0.86 us
    pallas_call x1, Pallas kernels, total(): pl.pallas_call(total_body, out_shape=(jax.ShapeDtypeStruct((points, full...  0.65 us
    ppermute x3, waiting for transfers between devices, over_line(): lax.ppermute(value, 'sub', [(p, partner(p, step, length)) for p in range(...  0.51 us
  transfers between devices with their start and end apart: 13, of which 7 were waited for; matrix products, arithmetic and copies ran while one was open for 0% of the time, Pallas kernels for 5%

profile of v3, /device:TPU:0, one launch (start us, length us, event | category | flops | bytes accessed | tf_op | source)
XLA Modules:
  0.0 25.5 jit_solution(4316152017758866567)
XLA Ops:
  0.6 0.0 copy-start.1
  0.7 0.9 %broadcast_divide_fusion = f32[32,512]{1,0:T(8,128)S(1)} fusion(f32[32,512]{1,0:T(8,128)} %param.4, f32[512]{0:T(512)} %param.5), kind=kLoop, calls=%fused_computation.1 | loop fusion | flops 16384 | bytes 133120 | tf_op jit(solution)/shard_map/div | solution.py:136
  1.5 0.1 pad_maximum_fusion.refs_0_.refs_4_
  1.6 4.0 %collective-permute-start.3 = (f32[32,640]{1,0:T(8,128)S(1)}, f32[32,640]{1,0:T(8,128)S(1)}, u32[]{:S(2)}, u32[]{:S(2)}) collective-permute-start(f32[32,640]{1,0:T(8,128)S(1)} %pad_maximum_fusion.refs_0_.refs_4_), channel_id=1, source_target_pairs={{0,2},{1,3},{2,0},{3,1},{4,6},{5,7},{6,4},{7,5},{8,10},{9,11},{10,... | collective-permute-start | bytes 245768 | tf_op jit(solution)/shard_map/ppermute | solution.py:45
  5.7 1.6 %collective-permute-start.6 = (f32[32,640]{1,0:T(8,128)S(1)}, f32[32,640]{1,0:T(8,128)S(1)}, u32[]{:S(2)}, u32[]{:S(2)}) collective-permute-start(f32[32,640]{1,0:T(8,128)S(1)} %pad_maximum_fusion.refs_0_.refs_4_), channel_id=1, source_target_pairs={{0,1},{1,0},{2,3},{3,2},{4,5},{5,4},{6,7},{7,6},{8,9},{9,8},{10,11... | collective-permute-start | bytes 245768 | tf_op jit(solution)/shard_map/ppermute | solution.py:45
  7.2 2.4 %collective-permute-start = (f32[32,640]{1,0:T(8,128)S(1)}, f32[32,640]{1,0:T(8,128)S(1)}, u32[]{:S(2)}, u32[]{:S(2)}) collective-permute-start(f32[32,640]{1,0:T(8,128)S(1)} %pad_maximum_fusion.refs_0_.refs_4_), channel_id=1, source_target_pairs={{0,24},{4,28},{8,16},{12,20},{16,8},{20,12},{24,0},{28,4},{1,25},{... | collective-permute-start | bytes 245768 | tf_op jit(solution)/shard_map/ppermute | solution.py:40
  9.7 0.5 %collective-permute-start.1 = (f32[32,640]{1,0:T(8,128)S(1)}, f32[32,640]{1,0:T(8,128)S(1)}, u32[]{:S(2)}, u32[]{:S(2)}) collective-permute-start(f32[32,640]{1,0:T(8,128)S(1)} %pad_maximum_fusion.refs_0_.refs_4_), channel_id=1, source_target_pairs={{0,16},{4,20},{8,24},{12,28},{16,0},{20,4},{24,8},{28,12},{1,17},{... | collective-permute-start | bytes 245768 | tf_op jit(solution)/shard_map/ppermute | solution.py:40
  10.2 0.0 collective-permute-done.3.refs_5_
  10.2 0.5 %collective-permute-start.4 = (f32[32,640]{1,0:T(8,128)S(1)}, f32[32,640]{1,0:T(8,128)S(1)}, u32[]{:S(2)}, u32[]{:S(2)}) collective-permute-start(f32[32,640]{1,0:T(8,128)S(1)} %collective-permute-done.3.refs_5_), channel_id=1, source_target_pairs={{0,1},{1,0},{2,3},{3,2},{4,5},{5,4},{6,7},{7,6},{8,9},{9,8},{10,11... | collective-permute-start | bytes 245768 | tf_op jit(solution)/shard_map/ppermute | solution.py:45
  10.6 1.5 %collective-permute-start.2 = (f32[32,640]{1,0:T(8,128)S(1)}, f32[32,640]{1,0:T(8,128)S(1)}, u32[]{:S(2)}, u32[]{:S(2)}) collective-permute-start(f32[32,640]{1,0:T(8,128)S(1)} %pad_maximum_fusion.refs_0_.refs_4_), channel_id=1, source_target_pairs={{0,8},{4,12},{8,0},{12,4},{16,24},{20,28},{24,16},{28,20},{1,9},{5... | collective-permute-start | bytes 245768 | tf_op jit(solution)/shard_map/ppermute | solution.py:40
  12.1 0.0 collective-permute-done.6.refs_6_
  12.1 0.0 collective-permute-start.7
  12.1 0.6 %collective-permute-done.refs_1_ = f32[32,640]{1,0:T(8,128)S(1)} collective-permute-done((f32[32,640]{1,0:T(8,128)S(1)}, f32[32,640]{1,0:T(8,128)S(1)}, u32[]{:S(2)}, u32[]{:S(2)}) %collective-permute-start) | collective-permute-done | bytes 81952 | tf_op jit(solution)/shard_map/ppermute | solution.py:40
  12.7 0.0 collective-permute-start.8
  12.7 1.4 %collective-permute-done.1.refs_2_ = f32[32,640]{1,0:T(8,128)S(1)} collective-permute-done((f32[32,640]{1,0:T(8,128)S(1)}, f32[32,640]{1,0:T(8,128)S(1)}, u32[]{:S(2)}, u32[]{:S(2)}) %collective-permute-start.1) | collective-permute-done | bytes 81952 | tf_op jit(solution)/shard_map/ppermute | solution.py:40
  14.1 0.0 collective-permute-start.9
  14.1 0.5 %collective-permute-done.4.refs_4_ = f32[32,640]{1,0:T(8,128)S(1)} collective-permute-done((f32[32,640]{1,0:T(8,128)S(1)}, f32[32,640]{1,0:T(8,128)S(1)}, u32[]{:S(2)}, u32[]{:S(2)}) %collective-permute-start.4) | collective-permute-done | bytes 81952 | tf_op jit(solution)/shard_map/ppermute | solution.py:45
  14.6 0.0 collective-permute-start.5
  14.6 0.4 %collective-permute-done.2.refs_3_ = f32[32,640]{1,0:T(8,128)S(1)} collective-permute-done((f32[32,640]{1,0:T(8,128)S(1)}, f32[32,640]{1,0:T(8,128)S(1)}, u32[]{:S(2)}, u32[]{:S(2)}) %collective-permute-start.2) | collective-permute-done | bytes 81952 | tf_op jit(solution)/shard_map/ppermute | solution.py:40
  15.1 0.0 collective-permute-done.7.refs_7_
  15.1 0.0 collective-permute-done.8.refs_8_
  15.1 0.3 %collective-permute-done.9.refs_9_ = f32[32,640]{1,0:T(8,128)S(1)} collective-permute-done((f32[32,640]{1,0:T(8,128)S(1)}, f32[32,640]{1,0:T(8,128)S(1)}, u32[]{:S(2)}, u32[]{:S(2)}) %collective-permute-start.9) | collective-permute-done | bytes 81952 | tf_op jit(solution)/shard_map/ppermute | solution.py:49
  15.4 1.3 %shard_map.59 = (f32[32,576]{1,0:T(8,128)S(1)}, f32[32,576]{1,0:T(8,128)S(1)}, f32[32,576]{1,0:T(8,128)S(1)}, f32[32,576]{1,0:T(8,128)S(1)}) custom-call(f32[32,640]{1,0:T(8,128)S(1)} %pad_maximum_fusion.refs_0_.refs_4_, f32[32,640]{1,0:T(8,128)S(1)} %collective-permute-done.refs_1_, f32[32,640]{1,0:T(8,128)S(1)} %collective-permute-done.1.refs_2_, ...), custom_call_target="tpu_custom_call" | custom-call | flops 358612992 | bytes 819200 | tf_op jit(solution)/shard_map/pallas_call | solution.py:98
  16.7 0.0 collective-permute-done.5.refs_5_
  16.7 0.9 %shard_map.60 = (f32[32,576]{1,0:T(8,128)S(1)}, f32[32,576]{1,0:T(8,128)S(1)}, f32[32,576]{1,0:T(8,128)S(1)}, f32[32,576]{1,0:T(8,128)S(1)}) custom-call(f32[32,640]{1,0:T(8,128)S(1)} %pad_maximum_fusion.refs_0_.refs_4_, f32[32,640]{1,0:T(8,128)S(1)} %collective-permute-done.refs_1_, f32[32,640]{1,0:T(8,128)S(1)} %collective-permute-done.1.refs_2_, ...), custom_call_target="tpu_custom_call" | custom-call | flops 119537664 | bytes 491520 | tf_op jit(solution)/shard_map/pallas_call | solution.py:98
  17.6 2.2 %collective-permute-start.10 = (f32[32,576]{1,0:T(8,128)S(1)}, f32[32,576]{1,0:T(8,128)S(1)}, u32[]{:S(2)}, u32[]{:S(2)}) collective-permute-start(f32[32,576]{1,0:T(8,128)S(1)} %get-tuple-element.15), channel_id=1, source_target_pairs={{24,0},{28,4},{16,8},{20,12},{8,16},{12,20},{0,24},{4,28},{25,1},{... | collective-permute-start | bytes 221192 | tf_op jit(solution)/shard_map/ppermute | solution.py:40
  19.8 0.5 %collective-permute-start.11 = (f32[32,576]{1,0:T(8,128)S(1)}, f32[32,576]{1,0:T(8,128)S(1)}, u32[]{:S(2)}, u32[]{:S(2)}) collective-permute-start(f32[32,576]{1,0:T(8,128)S(1)} %get-tuple-element.16), channel_id=1, source_target_pairs={{16,0},{20,4},{24,8},{28,12},{0,16},{4,20},{8,24},{12,28},{17,1},{... | collective-permute-start | bytes 221192 | tf_op jit(solution)/shard_map/ppermute | solution.py:40
  20.3 0.9 %collective-permute-start.12 = (f32[32,576]{1,0:T(8,128)S(1)}, f32[32,576]{1,0:T(8,128)S(1)}, u32[]{:S(2)}, u32[]{:S(2)}) collective-permute-start(f32[32,576]{1,0:T(8,128)S(1)} %get-tuple-element.17), channel_id=1, source_target_pairs={{8,0},{12,4},{0,8},{4,12},{24,16},{28,20},{16,24},{20,28},{9,1},{1... | collective-permute-start | bytes 221192 | tf_op jit(solution)/shard_map/ppermute | solution.py:40
  21.1 2.1 %collective-permute-done.10.refs_1_ = f32[32,576]{1,0:T(8,128)S(1)} collective-permute-done((f32[32,576]{1,0:T(8,128)S(1)}, f32[32,576]{1,0:T(8,128)S(1)}, u32[]{:S(2)}, u32[]{:S(2)}) %collective-permute-start.10) | collective-permute-done | bytes 73760 | tf_op jit(solution)/shard_map/ppermute | solution.py:40
  23.2 1.6 %collective-permute-done.11.refs_2_ = f32[32,576]{1,0:T(8,128)S(1)} collective-permute-done((f32[32,576]{1,0:T(8,128)S(1)}, f32[32,576]{1,0:T(8,128)S(1)}, u32[]{:S(2)}, u32[]{:S(2)}) %collective-permute-start.11) | collective-permute-done | bytes 73760 | tf_op jit(solution)/shard_map/ppermute | solution.py:40
  24.8 0.0 collective-permute-done.12.refs_3_
  24.8 0.6 %shard_map.61 = (f32[32,64]{1,0:T(8,128)}, f32[32,512]{1,0:T(8,128)}) custom-call(f32[32,576]{1,0:T(8,128)S(1)} %get-tuple-element.14.refs_0_, f32[32,576]{1,0:T(8,128)S(1)} %collective-permute-done.10.refs_1_, f32[32,576]{1,0:T(8,128)S(1)} %collective-permute-done.11.refs_2_, f32[32,576]{1,0:T(8,128)S(1)} %collective-permute-done.12.refs_3_), custom_call_target="tpu_custom_call" | custom-call | tf_op jit(solution)/shard_map/pallas_call | solution.py:121
  (3 shorter events, 0.0 us)
Async XLA Ops:
  0.6 0.9 %copy-start.1 = (f32[32,64]{1,0:T(8,128)S(1)}, f32[32,64]{1,0:T(8,128)}, u32[]{:S(2)}) copy-start(f32[32,64]{1,0:T(8,128)} %param.6) | copy-start | bytes 24580
  0.6 0.9 %copy-start = (f32[32,64]{1,0:T(8,128)S(1)}, f32[32,64]{1,0:T(8,128)}, u32[]{:S(2)}) copy-start(f32[32,64]{1,0:T(8,128)} %param.7) | copy-start | bytes 24580
  1.6 8.6 %collective-permute-start.3 = (f32[32,640]{1,0:T(8,128)S(1)}, f32[32,640]{1,0:T(8,128)S(1)}, u32[]{:S(2)}, u32[]{:S(2)}) collective-permute-start(f32[32,640]{1,0:T(8,128)S(1)} %pad_maximum_fusion.refs_0_.refs_4_), channel_id=1, source_target_pairs={{0,2},{1,3},{2,0},{3,1},{4,6},{5,7},{6,4},{7,5},{8,10},{9,11},{10,... | collective-permute-start | bytes 245768 | tf_op jit(solution)/shard_map/ppermute | solution.py:45
  5.7 6.4 %collective-permute-start.6 = (f32[32,640]{1,0:T(8,128)S(1)}, f32[32,640]{1,0:T(8,128)S(1)}, u32[]{:S(2)}, u32[]{:S(2)}) collective-permute-start(f32[32,640]{1,0:T(8,128)S(1)} %pad_maximum_fusion.refs_0_.refs_4_), channel_id=1, source_target_pairs={{0,1},{1,0},{2,3},{3,2},{4,5},{5,4},{6,7},{7,6},{8,9},{9,8},{10,11... | collective-permute-start | bytes 245768 | tf_op jit(solution)/shard_map/ppermute | solution.py:45
  7.2 5.4 %collective-permute-start = (f32[32,640]{1,0:T(8,128)S(1)}, f32[32,640]{1,0:T(8,128)S(1)}, u32[]{:S(2)}, u32[]{:S(2)}) collective-permute-start(f32[32,640]{1,0:T(8,128)S(1)} %pad_maximum_fusion.refs_0_.refs_4_), channel_id=1, source_target_pairs={{0,24},{4,28},{8,16},{12,20},{16,8},{20,12},{24,0},{28,4},{1,25},{... | collective-permute-start | bytes 245768 | tf_op jit(solution)/shard_map/ppermute | solution.py:40
  9.7 4.4 %collective-permute-start.1 = (f32[32,640]{1,0:T(8,128)S(1)}, f32[32,640]{1,0:T(8,128)S(1)}, u32[]{:S(2)}, u32[]{:S(2)}) collective-permute-start(f32[32,640]{1,0:T(8,128)S(1)} %pad_maximum_fusion.refs_0_.refs_4_), channel_id=1, source_target_pairs={{0,16},{4,20},{8,24},{12,28},{16,0},{20,4},{24,8},{28,12},{1,17},{... | collective-permute-start | bytes 245768 | tf_op jit(solution)/shard_map/ppermute | solution.py:40
  10.2 4.4 %collective-permute-start.4 = (f32[32,640]{1,0:T(8,128)S(1)}, f32[32,640]{1,0:T(8,128)S(1)}, u32[]{:S(2)}, u32[]{:S(2)}) collective-permute-start(f32[32,640]{1,0:T(8,128)S(1)} %collective-permute-done.3.refs_5_), channel_id=1, source_target_pairs={{0,1},{1,0},{2,3},{3,2},{4,5},{5,4},{6,7},{7,6},{8,9},{9,8},{10,11... | collective-permute-start | bytes 245768 | tf_op jit(solution)/shard_map/ppermute | solution.py:45
  10.6 4.4 %collective-permute-start.2 = (f32[32,640]{1,0:T(8,128)S(1)}, f32[32,640]{1,0:T(8,128)S(1)}, u32[]{:S(2)}, u32[]{:S(2)}) collective-permute-start(f32[32,640]{1,0:T(8,128)S(1)} %pad_maximum_fusion.refs_0_.refs_4_), channel_id=1, source_target_pairs={{0,8},{4,12},{8,0},{12,4},{16,24},{20,28},{24,16},{28,20},{1,9},{5... | collective-permute-start | bytes 245768 | tf_op jit(solution)/shard_map/ppermute | solution.py:40
  12.1 3.0 %collective-permute-start.7 = (f32[32,640]{1,0:T(8,128)S(1)}, f32[32,640]{1,0:T(8,128)S(1)}, u32[]{:S(2)}, u32[]{:S(2)}) collective-permute-start(f32[32,640]{1,0:T(8,128)S(1)} %pad_maximum_fusion.refs_0_.refs_4_), channel_id=1, source_target_pairs={{0,4},{4,0},{8,12},{12,8},{16,20},{20,16},{24,28},{28,24},{1,5},{5... | collective-permute-start | bytes 245768 | tf_op jit(solution)/shard_map/ppermute | solution.py:49
  12.7 2.4 %collective-permute-start.8 = (f32[32,640]{1,0:T(8,128)S(1)}, f32[32,640]{1,0:T(8,128)S(1)}, u32[]{:S(2)}, u32[]{:S(2)}) collective-permute-start(f32[32,640]{1,0:T(8,128)S(1)} %collective-permute-done.3.refs_5_), channel_id=1, source_target_pairs={{0,4},{4,0},{8,12},{12,8},{16,20},{20,16},{24,28},{28,24},{1,5},{5... | collective-permute-start | bytes 245768 | tf_op jit(solution)/shard_map/ppermute | solution.py:49
  14.1 1.3 %collective-permute-start.9 = (f32[32,640]{1,0:T(8,128)S(1)}, f32[32,640]{1,0:T(8,128)S(1)}, u32[]{:S(2)}, u32[]{:S(2)}) collective-permute-start(f32[32,640]{1,0:T(8,128)S(1)} %collective-permute-done.6.refs_6_), channel_id=1, source_target_pairs={{0,4},{4,0},{8,12},{12,8},{16,20},{20,16},{24,28},{28,24},{1,5},{5... | collective-permute-start | bytes 245768 | tf_op jit(solution)/shard_map/ppermute | solution.py:49
  14.6 2.1 %collective-permute-start.5 = (f32[32,640]{1,0:T(8,128)S(1)}, f32[32,640]{1,0:T(8,128)S(1)}, u32[]{:S(2)}, u32[]{:S(2)}) collective-permute-start(f32[32,640]{1,0:T(8,128)S(1)} %collective-permute-done.4.refs_4_), channel_id=1, source_target_pairs={{0,4},{4,0},{8,12},{12,8},{16,20},{20,16},{24,28},{28,24},{1,5},{5... | collective-permute-start | bytes 245768 | tf_op jit(solution)/shard_map/ppermute | solution.py:49
  17.6 5.6 %collective-permute-start.10 = (f32[32,576]{1,0:T(8,128)S(1)}, f32[32,576]{1,0:T(8,128)S(1)}, u32[]{:S(2)}, u32[]{:S(2)}) collective-permute-start(f32[32,576]{1,0:T(8,128)S(1)} %get-tuple-element.15), channel_id=1, source_target_pairs={{24,0},{28,4},{16,8},{20,12},{8,16},{12,20},{0,24},{4,28},{25,1},{... | collective-permute-start | bytes 221192 | tf_op jit(solution)/shard_map/ppermute | solution.py:40
  19.8 5.0 %collective-permute-start.11 = (f32[32,576]{1,0:T(8,128)S(1)}, f32[32,576]{1,0:T(8,128)S(1)}, u32[]{:S(2)}, u32[]{:S(2)}) collective-permute-start(f32[32,576]{1,0:T(8,128)S(1)} %get-tuple-element.16), channel_id=1, source_target_pairs={{16,0},{20,4},{24,8},{28,12},{0,16},{4,20},{8,24},{12,28},{17,1},{... | collective-permute-start | bytes 221192 | tf_op jit(solution)/shard_map/ppermute | solution.py:40
  20.3 4.5 %collective-permute-start.12 = (f32[32,576]{1,0:T(8,128)S(1)}, f32[32,576]{1,0:T(8,128)S(1)}, u32[]{:S(2)}, u32[]{:S(2)}) collective-permute-start(f32[32,576]{1,0:T(8,128)S(1)} %get-tuple-element.17), channel_id=1, source_target_pairs={{8,0},{12,4},{0,8},{4,12},{24,16},{28,20},{16,24},{20,28},{9,1},{1... | collective-permute-start | bytes 221192 | tf_op jit(solution)/shard_map/ppermute | solution.py:40

commit v4 on v3

v4 whole, which is shorter than its diff:
```python
import functools

import jax
import jax.numpy as jnp
from jax import lax
from jax.experimental import pallas as pl
from jax.experimental.pallas import tpu as pltpu
from jax.sharding import PartitionSpec as P

HIGH = lax.Precision.HIGHEST
ROWS_RULE = (((1,), (1,)), ((), ()))
PLAIN_RULE = (((1,), (0,)), ((), ()))
CORES = 2
LANES = 128
MIB = 2**20


def whole(count):
    return [pl.BlockSpec(memory_space=pltpu.VMEM)] * count


def dot(left, right, rule=PLAIN_RULE):
    return lax.dot_general(left, right, rule, precision=HIGH, preferred_element_type=jnp.float32)


def partner(position, step, length):
    if length & (length - 1) == 0:
        return position ^ step
    return (position + step) % length


def over_cores(value):
    return lax.ppermute(value, "blk", [(i, i ^ 1) for i in range(lax.axis_size("blk"))])


def to_chips(value, first, second, back=False):
    blocks, length = lax.axis_size("blk"), lax.axis_size("sub")
    pairs = []
    for b in range(blocks):
        place, core = b // CORES, b % CORES
        along_plane, along_line = (first, second)[core]
        there = partner(place, along_plane, blocks // CORES) * CORES + core
        pairs += [(b * length + s, there * length + partner(s, along_line, length)) for s in range(length)]
    return lax.ppermute(value, ("blk", "sub"), [(b, a) for a, b in pairs] if back else pairs)


def terms_body(count, mixed, mixed_columns, adds, width, core_ref, *refs):
    row_count, column_count = count
    rows = [ref[...] for ref in refs[:row_count]]
    columns = [ref[...] for ref in refs[row_count : row_count + column_count]]
    points = rows[0].shape[0]
    first = core_ref[0] == 0
    for place in range(1, row_count, 2):
        one, other = rows[place : place + 2]
        rows[place] = jnp.where(first, one, other)
        rows[place + 1] = jnp.where(first, other, one)
    if mixed:
        here, there = (ref[...] for ref in refs[row_count + column_count : row_count + column_count + 2])
        rows.append(jnp.where(first, here[:points], there[points:]))
        if mixed_columns:
            columns.append(jnp.where(first, there, here))
    operand_count = row_count + column_count + 2 * mixed
    sums = refs[operand_count : len(refs) - len(rows)]
    outs = refs[len(refs) - len(rows) :]
    rows, columns = jnp.concatenate(rows, axis=0), jnp.concatenate(columns, axis=0)
    probes = (rows.shape[1] - width) // 2
    row_scaled, column_scaled = rows[:, :width], columns[:, :width]
    row_norms = jnp.sum(row_scaled * row_scaled, axis=1, keepdims=True)
    column_norms = jnp.sum(column_scaled * column_scaled, axis=1, keepdims=True)
    column_norms = jnp.broadcast_to(column_norms, (column_norms.shape[0], LANES)).T[:1]
    inner = dot(row_scaled, column_scaled, ROWS_RULE)
    kernel = jnp.exp(-0.5 * (row_norms + column_norms - 2.0 * inner))
    column_probes = columns[:, width : width + probes]
    swapped = jnp.concatenate([columns[:, width + probes :], column_probes], axis=1)
    weight = kernel * dot(rows[:, width:], swapped, ROWS_RULE)
    product = dot(kernel, column_probes)
    gradient = dot(weight, column_scaled) - jnp.sum(weight, axis=1, keepdims=True) * row_scaled
    for place, out in enumerate(outs):
        part = slice(place * points, (place + 1) * points)
        if adds:
            out[:, :width] = sums[place][:, :width] + gradient[part]
            out[:, width:] = sums[place][:, width:] + product[part]
        else:
            out[:, :width] = gradient[part]
            out[:, width:] = product[part]


def terms(core, rows, columns, mixed, sums, width):
    points, full = rows[0].shape
    probes = (full - width) // 2
    row_count = len(rows) + bool(mixed)
    m, n = points * row_count, sum(p.shape[0] for p in columns) + (CORES * points if mixed and not sums else 0)
    operands = [*rows, *columns, *mixed, *(sums or ())]
    held = 4 * (8 * (m + n) * full + 8 * m * n)
    return pl.pallas_call(
        functools.partial(terms_body, (len(rows), len(columns)), bool(mixed), not sums, bool(sums), width),
        out_shape=[jax.ShapeDtypeStruct((points, width + probes), jnp.float32)] * row_count,
        in_specs=[pl.BlockSpec(memory_space=pltpu.SMEM)] + whole(len(operands)),
        out_specs=whole(row_count),
        compiler_params=pltpu.CompilerParams(vmem_limit_bytes=max(8 * MIB, held)),
        cost_estimate=pl.CostEstimate(
            flops=12 * m * n * (2 * width + 3 * probes), bytes_accessed=4 * (m + n) * full, transcendentals=m * n
        ),
    )(core, *operands)


def total_body(*refs):
    parts, (product, gradient) = refs[:-2], refs[-2:]
    total = parts[0][...]
    for part in parts[1:]:
        total = total + part[...]
    gradient[...] = total[:, : gradient.shape[1]]
    product[...] = total[:, gradient.shape[1] :]


def total(parts, width):
    points, full = parts[0].shape
    return pl.pallas_call(
        total_body,
        out_shape=(
            jax.ShapeDtypeStruct((points, full - width), jnp.float32),
            jax.ShapeDtypeStruct((points, width), jnp.float32),
        ),
        in_specs=whole(len(parts)),
        out_specs=tuple(whole(2)),
        compiler_params=pltpu.CompilerParams(vmem_limit_bytes=4 * MIB),
    )(*parts)


def in_twos(steps):
    return [(steps[i], steps[i + 1]) for i in range(0, len(steps) - 1, 2)]


def on_device(features, lengthscale, probes, cotangent):
    width, points = features.shape[1], features.shape[0]
    places, length = lax.axis_size("blk") // CORES, lax.axis_size("sub")
    core = (lax.axis_index("blk") % CORES).astype(jnp.int32).reshape(1)
    scaled = features / lengthscale[None, :]
    data = jnp.concatenate([scaled, probes, cotangent], axis=1)
    chip = jnp.concatenate([data, over_cores(data)], axis=0)
    line = [(0, step) for step in range(1, length)]
    plane = [(step, 0) for step in range(1, places)]
    rows, columns, mixed, ways, late = [data], [chip], [], [], []
    for first, second in in_twos(line):
        late.append(to_chips(chip, first, second))
    odd_line, odd_plane = line[len(line) // 2 * 2 :], plane[len(plane) // 2 * 2 :]
    if odd_line and odd_plane:
        got = to_chips(chip, odd_plane[0], odd_line[0])
        mixed = [got, over_cores(got)]
    elif odd_line:
        columns.append(to_chips(chip, odd_line[0], odd_line[0]))
    for first, second in in_twos(plane):
        got = to_chips(chip, second, first)
        rows += [got[:points], over_cores(got[points:])]
        ways += [(second, second), (first, first)]
    if odd_plane:
        ways.append((odd_plane[0], odd_plane[0]))
        if not mixed:
            rows.append(to_chips(data, odd_plane[0], odd_plane[0]))
    sums = terms(core, rows, columns, mixed, None, width)
    late, sums = lax.optimization_barrier((late, sums))
    if late:
        late += [over_cores(piece) for piece in late]
        sums = terms(core, rows, late, mixed, sums, width)
    own, *others = sums
    returns = list(zip(others, ways))
    back = [to_chips(part, *way, back=True) for part, way in returns[-1:] + returns[:-1]]
    return total([own] + back, width)


def solution(mesh):
    spec = P(("blk", "sub"), None)
    return jax.shard_map(
        on_device, mesh=mesh, in_specs=(spec, P(), spec, spec), out_specs=(spec, spec), check_vma=False
    )
```

time: 25.6 us -> 25.5 us (level)
  starting transfers between devices: 14 us -> 11.3 us
  waiting for transfers between devices: 6.96 us -> 9.63 us
    ppermute x9 -> x6, starting transfers between devices: 14 us -> 9.46 us  [to_chips(): lax.ppermute(value, ('blk', 'sub'), [(b, a) for a, b in pairs] if back el...]
    ppermute x4, waiting for transfers between devices: 0.32 us -> 2.88 us  [over_cores(): lax.ppermute(value, 'blk', [(i, i ^ 1) for i in range(lax.axis_size('blk'...]
    ppermute x4, starting transfers between devices: 0.01 us -> 1.89 us  [over_cores(): lax.ppermute(value, 'blk', [(i, i ^ 1) for i in range(lax.axis_size('blk'...]
    ppermute x9 -> x6, waiting for transfers between devices: 6.64 us -> 6.75 us  [to_chips(): lax.ppermute(value, ('blk', 'sub'), [(b, a) for a, b in pairs] if back el...]
  transfers between devices with their start and end apart: 13 -> 10, of which waited for: 7 -> 8; matrix products, arithmetic and copies ran while one was open for 0% -> 0% of each run, Pallas kernels for 5% -> 4%
where the time goes in v4:
time: 25.5 us; the launch traced here: 25.4 us
  starting transfers between devices  11.3 us (44%)
  waiting for transfers between devices  9.63 us (38%)
  Pallas kernels  2.65 us (10%)
  other arithmetic  1.02 us (4%)
  between operations  0.7 us (3%)
    ppermute x6, starting transfers between devices, to_chips(): lax.ppermute(value, ('blk', 'sub'), [(b, a) for a, b in pairs] if back el...  9.46 us
    ppermute x6, waiting for transfers between devices, to_chips(): lax.ppermute(value, ('blk', 'sub'), [(b, a) for a, b in pairs] if back el...  6.75 us
    ppermute x4, waiting for transfers between devices, over_cores(): lax.ppermute(value, 'blk', [(i, i ^ 1) for i in range(lax.axis_size('blk'...  2.88 us
    pallas_call x2, Pallas kernels, terms(): pl.pallas_call(functools.partial(terms_body, (len(rows), len(columns)), b...  2 us
    ppermute x4, starting transfers between devices, over_cores(): lax.ppermute(value, 'blk', [(i, i ^ 1) for i in range(lax.axis_size('blk'...  1.89 us
    div x1, other arithmetic, on_device(): scaled = features / lengthscale[None, :]  0.86 us
    pallas_call x1, Pallas kernels, total(): pl.pallas_call(total_body, out_shape=(jax.ShapeDtypeStruct((points, full...  0.65 us
  transfers between devices with their start and end apart: 10, of which 8 were waited for; matrix products, arithmetic and copies ran while one was open for 0% of the time, Pallas kernels for 4%

profile of v4, /device:TPU:0, one launch (start us, length us, event | category | flops | bytes accessed | tf_op | source)
XLA Modules:
  0.0 25.4 jit_solution(5138590725333486623)
XLA Ops:
  0.6 0.0 copy-start
  0.6 0.0 copy-start.1
  0.7 0.9 %broadcast_divide_fusion = f32[32,512]{1,0:T(8,128)S(1)} fusion(f32[32,512]{1,0:T(8,128)} %param.4, f32[512]{0:T(512)} %param.5), kind=kLoop, calls=%fused_computation.2 | loop fusion | flops 16384 | bytes 133120 | tf_op jit(solution)/shard_map/div | solution.py:138
  1.5 0.0 copy-done
  1.5 0.0 copy-done.1
  1.5 0.1 pad_maximum_fusion.1.refs_0_
  1.6 0.5 %collective-permute-start = (f32[32,640]{1,0:T(8,128)S(1)}, f32[32,640]{1,0:T(8,128)S(1)}, u32[]{:S(2)}, u32[]{:S(2)}) collective-permute-start(f32[32,640]{1,0:T(8,128)S(1)} %pad_maximum_fusion.1.refs_0_), channel_id=1, source_target_pairs={{0,4},{4,0},{8,12},{12,8},{16,20},{20,16},{24,28},{28,24},{1,5},{5... | collective-permute-start | bytes 245768 | tf_op jit(solution)/shard_map/ppermute | solution.py:33
  2.1 0.9 %collective-permute-done = f32[32,640]{1,0:T(8,128)S(1)} collective-permute-done((f32[32,640]{1,0:T(8,128)S(1)}, f32[32,640]{1,0:T(8,128)S(1)}, u32[]{:S(2)}, u32[]{:S(2)}) %collective-permute-start) | collective-permute-done | bytes 81952 | tf_op jit(solution)/shard_map/ppermute | solution.py:33
  3.0 0.1 pad_maximum_fusion.refs_3_
  3.1 3.8 %collective-permute-start.4 = (f32[64,640]{1,0:T(8,128)S(1)}, f32[64,640]{1,0:T(8,128)S(1)}, u32[]{:S(2)}, u32[]{:S(2)}) collective-permute-start(f32[64,640]{1,0:T(8,128)S(1)} %pad_maximum_fusion.refs_3_), channel_id=1, source_target_pairs={{0,24},{1,25},{2,26},{3,27},{4,7},{5,6},{6,5},{7,4},{8,16},{9,17},... | collective-permute-start | bytes 491528 | tf_op jit(solution)/shard_map/ppermute | solution.py:44
  6.9 0.5 %collective-permute-start.1 = (f32[64,640]{1,0:T(8,128)S(1)}, f32[64,640]{1,0:T(8,128)S(1)}, u32[]{:S(2)}, u32[]{:S(2)}) collective-permute-start(f32[64,640]{1,0:T(8,128)S(1)} %pad_maximum_fusion.refs_3_), channel_id=1, source_target_pairs={{0,16},{1,17},{2,18},{3,19},{4,12},{5,13},{6,14},{7,15},{8,24},{9,... | collective-permute-start | bytes 491528 | tf_op jit(solution)/shard_map/ppermute | solution.py:44
  7.4 1.6 %collective-permute-start.3 = (f32[64,640]{1,0:T(8,128)S(1)}, f32[64,640]{1,0:T(8,128)S(1)}, u32[]{:S(2)}, u32[]{:S(2)}) collective-permute-start(f32[64,640]{1,0:T(8,128)S(1)} %pad_maximum_fusion.refs_3_), channel_id=1, source_target_pairs={{0,1},{1,0},{2,3},{3,2},{4,6},{5,7},{6,4},{7,5},{8,9},{9,8},{10,11... | collective-permute-start | bytes 491528 | tf_op jit(solution)/shard_map/ppermute | solution.py:44
  9.0 1.2 %collective-permute-done.4.refs_4_.refs_5_ = f32[64,640]{1,0:T(8,128)S(1)} collective-permute-done((f32[64,640]{1,0:T(8,128)S(1)}, f32[64,640]{1,0:T(8,128)S(1)}, u32[]{:S(2)}, u32[]{:S(2)}) %collective-permute-start.4) | collective-permute-done | bytes 163872 | tf_op jit(solution)/shard_map/ppermute | solution.py:44
  10.2 0.5 %collective-permute-start.5 = (f32[64,640]{1,0:T(8,128)S(1)}, f32[64,640]{1,0:T(8,128)S(1)}, u32[]{:S(2)}, u32[]{:S(2)}) collective-permute-start(f32[64,640]{1,0:T(8,128)S(1)} %collective-permute-done.4.refs_4_.refs_5_), channel_id=1, source_target_pairs={{0,4},{4,0},{8,12},{12,8},{16,20},{20,16},{24,28},{28,24},{1,5},{5... | collective-permute-start | bytes 491528 | tf_op jit(solution)/shard_map/ppermute | solution.py:33
  10.7 1.5 %collective-permute-done.1 = f32[64,640]{1,0:T(8,128)S(1)} collective-permute-done((f32[64,640]{1,0:T(8,128)S(1)}, f32[64,640]{1,0:T(8,128)S(1)}, u32[]{:S(2)}, u32[]{:S(2)}) %collective-permute-start.1) | collective-permute-done | bytes 163872 | tf_op jit(solution)/shard_map/ppermute | solution.py:44
  12.2 0.4 %collective-permute-start.2 = (f32[32,640]{1,0:T(8,128)S(1)}, f32[32,640]{1,0:T(8,128)S(1)}, u32[]{:S(2)}, u32[]{:S(2)}) collective-permute-start(f32[32,640]{1,0:T(8,128)S(1)} %get-tuple-element.28), channel_id=1, source_target_pairs={{0,4},{4,0},{8,12},{12,8},{16,20},{20,16},{24,28},{28,24},{1,5},{5... | collective-permute-start | bytes 245768 | tf_op jit(solution)/shard_map/ppermute | solution.py:33
  12.7 0.9 %collective-permute-done.2.refs_2_ = f32[32,640]{1,0:T(8,128)S(1)} collective-permute-done((f32[32,640]{1,0:T(8,128)S(1)}, f32[32,640]{1,0:T(8,128)S(1)}, u32[]{:S(2)}, u32[]{:S(2)}) %collective-permute-start.2) | collective-permute-done | bytes 81952 | tf_op jit(solution)/shard_map/ppermute | solution.py:33
  13.6 0.0 collective-permute-done.5.refs_5_.refs_6_
  13.6 1.0 %shard_map.59 = (f32[32,576]{1,0:T(8,128)S(1)}, f32[32,576]{1,0:T(8,128)S(1)}, f32[32,576]{1,0:T(8,128)S(1)}, f32[32,576]{1,0:T(8,128)S(1)}) custom-call(s32[1]{0:T(128)} %bitcast.core_ref, f32[32,640]{1,0:T(8,128)S(1)} %pad_maximum_fusion.1.refs_0_, f32[32,640]{1,0:T(8,128)S(1)} %get-tuple-element.29.refs_1_, f32[32,640]{1,0:T(8,128)S(1)} %collective-permute-done.2.refs_2_, ...), custom_call_target="tpu_custom_call" | custom-call | flops 239075328 | bytes 655360 | tf_op jit(solution)/shard_map/pallas_call | solution.py:95
  14.6 0.0 collective-permute-done.3.refs_3_
  14.6 0.4 %collective-permute-start.6 = (f32[64,640]{1,0:T(8,128)S(1)}, f32[64,640]{1,0:T(8,128)S(1)}, u32[]{:S(2)}, u32[]{:S(2)}) collective-permute-start(f32[64,640]{1,0:T(8,128)S(1)} %collective-permute-done.3.refs_3_), channel_id=1, source_target_pairs={{0,4},{4,0},{8,12},{12,8},{16,20},{20,16},{24,28},{28,24},{1,5},{5... | collective-permute-start | bytes 491528 | tf_op jit(solution)/shard_map/ppermute | solution.py:33
  15.0 1.0 %collective-permute-done.6.refs_4_ = f32[64,640]{1,0:T(8,128)S(1)} collective-permute-done((f32[64,640]{1,0:T(8,128)S(1)}, f32[64,640]{1,0:T(8,128)S(1)}, u32[]{:S(2)}, u32[]{:S(2)}) %collective-permute-start.6) | collective-permute-done | bytes 163872 | tf_op jit(solution)/shard_map/ppermute | solution.py:33
  16.1 1.0 %shard_map.60 = (f32[32,576]{1,0:T(8,128)S(1)}, f32[32,576]{1,0:T(8,128)S(1)}, f32[32,576]{1,0:T(8,128)S(1)}, f32[32,576]{1,0:T(8,128)S(1)}) custom-call(s32[1]{0:T(128)} %bitcast.core_ref, f32[32,640]{1,0:T(8,128)S(1)} %pad_maximum_fusion.1.refs_0_, f32[32,640]{1,0:T(8,128)S(1)} %get-tuple-element.29.refs_1_, f32[32,640]{1,0:T(8,128)S(1)} %collective-permute-done.2.refs_2_, ...), custom_call_target="tpu_custom_call" | custom-call | flops 239075328 | bytes 655360 | tf_op jit(solution)/shard_map/pallas_call | solution.py:95
  17.1 2.5 %collective-permute-start.7 = (f32[32,576]{1,0:T(8,128)S(1)}, f32[32,576]{1,0:T(8,128)S(1)}, u32[]{:S(2)}, u32[]{:S(2)}) collective-permute-start(f32[32,576]{1,0:T(8,128)S(1)} %get-tuple-element.25), channel_id=1, source_target_pairs={{24,0},{25,1},{26,2},{27,3},{28,4},{29,5},{30,6},{31,7},{16,8},{17... | collective-permute-start | bytes 221192 | tf_op jit(solution)/shard_map/ppermute | solution.py:44
  19.6 0.7 %collective-permute-start.8 = (f32[32,576]{1,0:T(8,128)S(1)}, f32[32,576]{1,0:T(8,128)S(1)}, u32[]{:S(2)}, u32[]{:S(2)}) collective-permute-start(f32[32,576]{1,0:T(8,128)S(1)} %get-tuple-element.26), channel_id=1, source_target_pairs={{16,0},{17,1},{18,2},{19,3},{20,4},{21,5},{22,6},{23,7},{24,8},{25... | collective-permute-start | bytes 221192 | tf_op jit(solution)/shard_map/ppermute | solution.py:44
  20.3 0.4 %collective-permute-start.9 = (f32[32,576]{1,0:T(8,128)S(1)}, f32[32,576]{1,0:T(8,128)S(1)}, u32[]{:S(2)}, u32[]{:S(2)}) collective-permute-start(f32[32,576]{1,0:T(8,128)S(1)} %get-tuple-element.27), channel_id=1, source_target_pairs={{8,0},{9,1},{10,2},{11,3},{12,4},{13,5},{14,6},{15,7},{0,8},{1,9},... | collective-permute-start | bytes 221192 | tf_op jit(solution)/shard_map/ppermute | solution.py:44
  20.7 2.2 %collective-permute-done.7.refs_1_ = f32[32,576]{1,0:T(8,128)S(1)} collective-permute-done((f32[32,576]{1,0:T(8,128)S(1)}, f32[32,576]{1,0:T(8,128)S(1)}, u32[]{:S(2)}, u32[]{:S(2)}) %collective-permute-start.7) | collective-permute-done | bytes 73760 | tf_op jit(solution)/shard_map/ppermute | solution.py:44
  22.8 1.7 %collective-permute-done.8.refs_2_ = f32[32,576]{1,0:T(8,128)S(1)} collective-permute-done((f32[32,576]{1,0:T(8,128)S(1)}, f32[32,576]{1,0:T(8,128)S(1)}, u32[]{:S(2)}, u32[]{:S(2)}) %collective-permute-start.8) | collective-permute-done | bytes 73760 | tf_op jit(solution)/shard_map/ppermute | solution.py:44
  24.5 0.2 collective-permute-done.9.refs_3_
  24.7 0.7 %shard_map.61 = (f32[32,64]{1,0:T(8,128)}, f32[32,512]{1,0:T(8,128)}) custom-call(f32[32,576]{1,0:T(8,128)S(1)} %get-tuple-element.24.refs_0_, f32[32,576]{1,0:T(8,128)S(1)} %collective-permute-done.7.refs_1_, f32[32,576]{1,0:T(8,128)S(1)} %collective-permute-done.8.refs_2_, f32[32,576]{1,0:T(8,128)S(1)} %collective-permute-done.9.refs_3_), custom_call_target="tpu_custom_call" | custom-call | tf_op jit(solution)/shard_map/pallas_call | solution.py:118
  (1 shorter events, 0.0 us)
Async XLA Ops:
  0.6 0.9 %copy-start = (f32[32,64]{1,0:T(8,128)S(1)}, f32[32,64]{1,0:T(8,128)}, u32[]{:S(2)}) copy-start(f32[32,64]{1,0:T(8,128)} %param.7) | copy-start | bytes 24580
  0.6 0.9 %copy-start.1 = (f32[32,64]{1,0:T(8,128)S(1)}, f32[32,64]{1,0:T(8,128)}, u32[]{:S(2)}) copy-start(f32[32,64]{1,0:T(8,128)} %param.6) | copy-start | bytes 24580
  1.6 1.4 %collective-permute-start = (f32[32,640]{1,0:T(8,128)S(1)}, f32[32,640]{1,0:T(8,128)S(1)}, u32[]{:S(2)}, u32[]{:S(2)}) collective-permute-start(f32[32,640]{1,0:T(8,128)S(1)} %pad_maximum_fusion.1.refs_0_), channel_id=1, source_target_pairs={{0,4},{4,0},{8,12},{12,8},{16,20},{20,16},{24,28},{28,24},{1,5},{5... | collective-permute-start | bytes 245768 | tf_op jit(solution)/shard_map/ppermute | solution.py:33
  3.1 7.1 %collective-permute-start.4 = (f32[64,640]{1,0:T(8,128)S(1)}, f32[64,640]{1,0:T(8,128)S(1)}, u32[]{:S(2)}, u32[]{:S(2)}) collective-permute-start(f32[64,640]{1,0:T(8,128)S(1)} %pad_maximum_fusion.refs_3_), channel_id=1, source_target_pairs={{0,24},{1,25},{2,26},{3,27},{4,7},{5,6},{6,5},{7,4},{8,16},{9,17},... | collective-permute-start | bytes 491528 | tf_op jit(solution)/shard_map/ppermute | solution.py:44
  6.9 5.3 %collective-permute-start.1 = (f32[64,640]{1,0:T(8,128)S(1)}, f32[64,640]{1,0:T(8,128)S(1)}, u32[]{:S(2)}, u32[]{:S(2)}) collective-permute-start(f32[64,640]{1,0:T(8,128)S(1)} %pad_maximum_fusion.refs_3_), channel_id=1, source_target_pairs={{0,16},{1,17},{2,18},{3,19},{4,12},{5,13},{6,14},{7,15},{8,24},{9,... | collective-permute-start | bytes 491528 | tf_op jit(solution)/shard_map/ppermute | solution.py:44
  7.4 7.2 %collective-permute-start.3 = (f32[64,640]{1,0:T(8,128)S(1)}, f32[64,640]{1,0:T(8,128)S(1)}, u32[]{:S(2)}, u32[]{:S(2)}) collective-permute-start(f32[64,640]{1,0:T(8,128)S(1)} %pad_maximum_fusion.refs_3_), channel_id=1, source_target_pairs={{0,1},{1,0},{2,3},{3,2},{4,6},{5,7},{6,4},{7,5},{8,9},{9,8},{10,11... | collective-permute-start | bytes 491528 | tf_op jit(solution)/shard_map/ppermute | solution.py:44
  10.2 3.4 %collective-permute-start.5 = (f32[64,640]{1,0:T(8,128)S(1)}, f32[64,640]{1,0:T(8,128)S(1)}, u32[]{:S(2)}, u32[]{:S(2)}) collective-permute-start(f32[64,640]{1,0:T(8,128)S(1)} %collective-permute-done.4.refs_4_.refs_5_), channel_id=1, source_target_pairs={{0,4},{4,0},{8,12},{12,8},{16,20},{20,16},{24,28},{28,24},{1,5},{5... | collective-permute-start | bytes 491528 | tf_op jit(solution)/shard_map/ppermute | solution.py:33
  12.2 1.4 %collective-permute-start.2 = (f32[32,640]{1,0:T(8,128)S(1)}, f32[32,640]{1,0:T(8,128)S(1)}, u32[]{:S(2)}, u32[]{:S(2)}) collective-permute-start(f32[32,640]{1,0:T(8,128)S(1)} %get-tuple-element.28), channel_id=1, source_target_pairs={{0,4},{4,0},{8,12},{12,8},{16,20},{20,16},{24,28},{28,24},{1,5},{5... | collective-permute-start | bytes 245768 | tf_op jit(solution)/shard_map/ppermute | solution.py:33
  14.6 1.5 %collective-permute-start.6 = (f32[64,640]{1,0:T(8,128)S(1)}, f32[64,640]{1,0:T(8,128)S(1)}, u32[]{:S(2)}, u32[]{:S(2)}) collective-permute-start(f32[64,640]{1,0:T(8,128)S(1)} %collective-permute-done.3.refs_3_), channel_id=1, source_target_pairs={{0,4},{4,0},{8,12},{12,8},{16,20},{20,16},{24,28},{28,24},{1,5},{5... | collective-permute-start | bytes 491528 | tf_op jit(solution)/shard_map/ppermute | solution.py:33
  17.1 5.7 %collective-permute-start.7 = (f32[32,576]{1,0:T(8,128)S(1)}, f32[32,576]{1,0:T(8,128)S(1)}, u32[]{:S(2)}, u32[]{:S(2)}) collective-permute-start(f32[32,576]{1,0:T(8,128)S(1)} %get-tuple-element.25), channel_id=1, source_target_pairs={{24,0},{25,1},{26,2},{27,3},{28,4},{29,5},{30,6},{31,7},{16,8},{17... | collective-permute-start | bytes 221192 | tf_op jit(solution)/shard_map/ppermute | solution.py:44
  19.6 4.9 %collective-permute-start.8 = (f32[32,576]{1,0:T(8,128)S(1)}, f32[32,576]{1,0:T(8,128)S(1)}, u32[]{:S(2)}, u32[]{:S(2)}) collective-permute-start(f32[32,576]{1,0:T(8,128)S(1)} %get-tuple-element.26), channel_id=1, source_target_pairs={{16,0},{17,1},{18,2},{19,3},{20,4},{21,5},{22,6},{23,7},{24,8},{25... | collective-permute-start | bytes 221192 | tf_op jit(solution)/shard_map/ppermute | solution.py:44
  20.3 4.4 %collective-permute-start.9 = (f32[32,576]{1,0:T(8,128)S(1)}, f32[32,576]{1,0:T(8,128)S(1)}, u32[]{:S(2)}, u32[]{:S(2)}) collective-permute-start(f32[32,576]{1,0:T(8,128)S(1)} %get-tuple-element.27), channel_id=1, source_target_pairs={{8,0},{9,1},{10,2},{11,3},{12,4},{13,5},{14,6},{15,7},{0,8},{1,9},... | collective-permute-start | bytes 221192 | tf_op jit(solution)/shard_map/ppermute | solution.py:44

commit v5 on v4

--- a/solution.py
+++ b/solution.py
@@ -160,8 +160,9 @@
     sums = terms(core, rows, columns, mixed, None, width)
     late, sums = lax.optimization_barrier((late, sums))
     if late:
-        late += [over_cores(piece) for piece in late]
+        swapped = [over_cores(piece) for piece in late]
         sums = terms(core, rows, late, mixed, sums, width)
+        sums = terms(core, rows, swapped, mixed, sums, width)
     own, *others = sums
     returns = list(zip(others, ways))
     back = [to_chips(part, *way, back=True) for part, way in returns[-1:] + returns[:-1]]

time: 25.5 us -> 25.4 us (level)
  waiting for transfers between devices: 9.63 us -> 8.76 us
  Pallas kernels: 2.65 us -> 3.36 us
    ppermute x4, waiting for transfers between devices: 2.88 us -> 2.01 us  [over_cores(): lax.ppermute(value, 'blk', [(i, i ^ 1) for i in range(lax.axis_size('blk'...]
    pallas_call x2 -> x3, Pallas kernels: 2 us -> 2.71 us  [terms(): pl.pallas_call(functools.partial(terms_body, (len(rows), len(columns)), b...]
  transfers between devices with their start and end apart: 10 -> 10, of which waited for: 8 -> 8; matrix products, arithmetic and copies ran while one was open for 0% -> 0% of each run, Pallas kernels for 4% -> 7%
where the time goes in v5:
time: 25.4 us; the launch traced here: 25.2 us
  starting transfers between devices  11.3 us (44%)
  waiting for transfers between devices  8.76 us (34%)
  Pallas kernels  3.36 us (13%)
  other arithmetic  1.02 us (4%)
  between operations  0.71 us (3%)
    ppermute x6, starting transfers between devices, to_chips(): lax.ppermute(value, ('blk', 'sub'), [(b, a) for a, b in pairs] if back el...  9.46 us
    ppermute x6, waiting for transfers between devices, to_chips(): lax.ppermute(value, ('blk', 'sub'), [(b, a) for a, b in pairs] if back el...  6.75 us
    pallas_call x3, Pallas kernels, terms(): pl.pallas_call(functools.partial(terms_body, (len(rows), len(columns)), b...  2.71 us
    ppermute x4, waiting for transfers between devices, over_cores(): lax.ppermute(value, 'blk', [(i, i ^ 1) for i in range(lax.axis_size('blk'...  2.01 us
    ppermute x4, starting transfers between devices, over_cores(): lax.ppermute(value, 'blk', [(i, i ^ 1) for i in range(lax.axis_size('blk'...  1.89 us
    div x1, other arithmetic, on_device(): scaled = features / lengthscale[None, :]  0.86 us
    pallas_call x1, Pallas kernels, total(): pl.pallas_call(total_body, out_shape=(jax.ShapeDtypeStruct((points, full...  0.65 us
  transfers between devices with their start and end apart: 10, of which 8 were waited for; matrix products, arithmetic and copies ran while one was open for 0% of the time, Pallas kernels for 7%

profile of v5, /device:TPU:0, one launch (start us, length us, event | category | flops | bytes accessed | tf_op | source)
XLA Modules:
  0.0 25.2 jit_solution(976253926653818482)
XLA Ops:
  0.6 0.0 copy-start
  0.6 0.0 copy-start.1
  0.7 0.9 %broadcast_divide_fusion = f32[32,512]{1,0:T(8,128)S(1)} fusion(f32[32,512]{1,0:T(8,128)} %param.4, f32[512]{0:T(512)} %param.5), kind=kLoop, calls=%fused_computation.2 | loop fusion | flops 16384 | bytes 133120 | tf_op jit(solution)/shard_map/div | solution.py:138
  1.5 0.0 copy-done
  1.5 0.0 copy-done.1
  1.5 0.1 pad_maximum_fusion.1.refs_0_
  1.6 0.5 %collective-permute-start = (f32[32,640]{1,0:T(8,128)S(1)}, f32[32,640]{1,0:T(8,128)S(1)}, u32[]{:S(2)}, u32[]{:S(2)}) collective-permute-start(f32[32,640]{1,0:T(8,128)S(1)} %pad_maximum_fusion.1.refs_0_), channel_id=1, source_target_pairs={{0,4},{4,0},{8,12},{12,8},{16,20},{20,16},{24,28},{28,24},{1,5},{5... | collective-permute-start | bytes 245768 | tf_op jit(solution)/shard_map/ppermute | solution.py:33
  2.1 0.9 %collective-permute-done = f32[32,640]{1,0:T(8,128)S(1)} collective-permute-done((f32[32,640]{1,0:T(8,128)S(1)}, f32[32,640]{1,0:T(8,128)S(1)}, u32[]{:S(2)}, u32[]{:S(2)}) %collective-permute-start) | collective-permute-done | bytes 81952 | tf_op jit(solution)/shard_map/ppermute | solution.py:33
  3.0 0.1 pad_maximum_fusion.refs_3_
  3.1 3.8 %collective-permute-start.4 = (f32[64,640]{1,0:T(8,128)S(1)}, f32[64,640]{1,0:T(8,128)S(1)}, u32[]{:S(2)}, u32[]{:S(2)}) collective-permute-start(f32[64,640]{1,0:T(8,128)S(1)} %pad_maximum_fusion.refs_3_), channel_id=1, source_target_pairs={{0,24},{1,25},{2,26},{3,27},{4,7},{5,6},{6,5},{7,4},{8,16},{9,17},... | collective-permute-start | bytes 491528 | tf_op jit(solution)/shard_map/ppermute | solution.py:44
  6.9 0.5 %collective-permute-start.1 = (f32[64,640]{1,0:T(8,128)S(1)}, f32[64,640]{1,0:T(8,128)S(1)}, u32[]{:S(2)}, u32[]{:S(2)}) collective-permute-start(f32[64,640]{1,0:T(8,128)S(1)} %pad_maximum_fusion.refs_3_), channel_id=1, source_target_pairs={{0,16},{1,17},{2,18},{3,19},{4,12},{5,13},{6,14},{7,15},{8,24},{9,... | collective-permute-start | bytes 491528 | tf_op jit(solution)/shard_map/ppermute | solution.py:44
  7.4 1.6 %collective-permute-start.3 = (f32[64,640]{1,0:T(8,128)S(1)}, f32[64,640]{1,0:T(8,128)S(1)}, u32[]{:S(2)}, u32[]{:S(2)}) collective-permute-start(f32[64,640]{1,0:T(8,128)S(1)} %pad_maximum_fusion.refs_3_), channel_id=1, source_target_pairs={{0,1},{1,0},{2,3},{3,2},{4,6},{5,7},{6,4},{7,5},{8,9},{9,8},{10,11... | collective-permute-start | bytes 491528 | tf_op jit(solution)/shard_map/ppermute | solution.py:44
  9.0 1.2 %collective-permute-done.4.refs_4_ = f32[64,640]{1,0:T(8,128)S(1)} collective-permute-done((f32[64,640]{1,0:T(8,128)S(1)}, f32[64,640]{1,0:T(8,128)S(1)}, u32[]{:S(2)}, u32[]{:S(2)}) %collective-permute-start.4) | collective-permute-done | bytes 163872 | tf_op jit(solution)/shard_map/ppermute | solution.py:44
  10.2 0.5 %collective-permute-start.5 = (f32[64,640]{1,0:T(8,128)S(1)}, f32[64,640]{1,0:T(8,128)S(1)}, u32[]{:S(2)}, u32[]{:S(2)}) collective-permute-start(f32[64,640]{1,0:T(8,128)S(1)} %collective-permute-done.4.refs_4_), channel_id=1, source_target_pairs={{0,4},{4,0},{8,12},{12,8},{16,20},{20,16},{24,28},{28,24},{1,5},{5... | collective-permute-start | bytes 491528 | tf_op jit(solution)/shard_map/ppermute | solution.py:33
  10.7 1.5 %collective-permute-done.1 = f32[64,640]{1,0:T(8,128)S(1)} collective-permute-done((f32[64,640]{1,0:T(8,128)S(1)}, f32[64,640]{1,0:T(8,128)S(1)}, u32[]{:S(2)}, u32[]{:S(2)}) %collective-permute-start.1) | collective-permute-done | bytes 163872 | tf_op jit(solution)/shard_map/ppermute | solution.py:44
  12.2 0.4 %collective-permute-start.2 = (f32[32,640]{1,0:T(8,128)S(1)}, f32[32,640]{1,0:T(8,128)S(1)}, u32[]{:S(2)}, u32[]{:S(2)}) collective-permute-start(f32[32,640]{1,0:T(8,128)S(1)} %get-tuple-element.36), channel_id=1, source_target_pairs={{0,4},{4,0},{8,12},{12,8},{16,20},{20,16},{24,28},{28,24},{1,5},{5... | collective-permute-start | bytes 245768 | tf_op jit(solution)/shard_map/ppermute | solution.py:33
  12.7 0.9 %collective-permute-done.2.refs_2_ = f32[32,640]{1,0:T(8,128)S(1)} collective-permute-done((f32[32,640]{1,0:T(8,128)S(1)}, f32[32,640]{1,0:T(8,128)S(1)}, u32[]{:S(2)}, u32[]{:S(2)}) %collective-permute-start.2) | collective-permute-done | bytes 81952 | tf_op jit(solution)/shard_map/ppermute | solution.py:33
  13.6 0.0 collective-permute-done.5.refs_5_
  13.6 1.0 %shard_map.59 = (f32[32,576]{1,0:T(8,128)S(1)}, f32[32,576]{1,0:T(8,128)S(1)}, f32[32,576]{1,0:T(8,128)S(1)}, f32[32,576]{1,0:T(8,128)S(1)}) custom-call(s32[1]{0:T(128)} %bitcast.core_ref, f32[32,640]{1,0:T(8,128)S(1)} %pad_maximum_fusion.1.refs_0_, f32[32,640]{1,0:T(8,128)S(1)} %get-tuple-element.37.refs_1_, f32[32,640]{1,0:T(8,128)S(1)} %collective-permute-done.2.refs_2_, ...), custom_call_target="tpu_custom_call" | custom-call | flops 239075328 | bytes 655360 | tf_op jit(solution)/shard_map/pallas_call | solution.py:95
  14.6 0.0 collective-permute-done.3.refs_3_
  14.6 0.4 %collective-permute-start.6 = (f32[64,640]{1,0:T(8,128)S(1)}, f32[64,640]{1,0:T(8,128)S(1)}, u32[]{:S(2)}, u32[]{:S(2)}) collective-permute-start(f32[64,640]{1,0:T(8,128)S(1)} %collective-permute-done.3.refs_3_), channel_id=1, source_target_pairs={{0,4},{4,0},{8,12},{12,8},{16,20},{20,16},{24,28},{28,24},{1,5},{5... | collective-permute-start | bytes 491528 | tf_op jit(solution)/shard_map/ppermute | solution.py:33
  15.0 0.9 %shard_map.60 = (f32[32,576]{1,0:T(8,128)S(1)}, f32[32,576]{1,0:T(8,128)S(1)}, f32[32,576]{1,0:T(8,128)S(1)}, f32[32,576]{1,0:T(8,128)S(1)}) custom-call(s32[1]{0:T(128)} %bitcast.core_ref, f32[32,640]{1,0:T(8,128)S(1)} %pad_maximum_fusion.1.refs_0_, f32[32,640]{1,0:T(8,128)S(1)} %get-tuple-element.37.refs_1_, f32[32,640]{1,0:T(8,128)S(1)} %collective-permute-done.2.refs_2_, ...), custom_call_target="tpu_custom_call" | custom-call | flops 119537664 | bytes 491520 | tf_op jit(solution)/shard_map/pallas_call | solution.py:95
  15.9 0.2 collective-permute-done.6.refs_3_
  16.1 0.9 %shard_map.61 = (f32[32,576]{1,0:T(8,128)S(1)}, f32[32,576]{1,0:T(8,128)S(1)}, f32[32,576]{1,0:T(8,128)S(1)}, f32[32,576]{1,0:T(8,128)S(1)}) custom-call(s32[1]{0:T(128)} %bitcast.core_ref, f32[32,640]{1,0:T(8,128)S(1)} %pad_maximum_fusion.1.refs_0_, f32[32,640]{1,0:T(8,128)S(1)} %get-tuple-element.37.refs_1_, f32[32,640]{1,0:T(8,128)S(1)} %collective-permute-done.2.refs_2_, ...), custom_call_target="tpu_custom_call" | custom-call | flops 119537664 | bytes 491520 | tf_op jit(solution)/shard_map/pallas_call | solution.py:95
  16.9 2.5 %collective-permute-start.7 = (f32[32,576]{1,0:T(8,128)S(1)}, f32[32,576]{1,0:T(8,128)S(1)}, u32[]{:S(2)}, u32[]{:S(2)}) collective-permute-start(f32[32,576]{1,0:T(8,128)S(1)} %get-tuple-element.33), channel_id=1, source_target_pairs={{24,0},{25,1},{26,2},{27,3},{28,4},{29,5},{30,6},{31,7},{16,8},{17... | collective-permute-start | bytes 221192 | tf_op jit(solution)/shard_map/ppermute | solution.py:44
  19.5 0.7 %collective-permute-start.8 = (f32[32,576]{1,0:T(8,128)S(1)}, f32[32,576]{1,0:T(8,128)S(1)}, u32[]{:S(2)}, u32[]{:S(2)}) collective-permute-start(f32[32,576]{1,0:T(8,128)S(1)} %get-tuple-element.34), channel_id=1, source_target_pairs={{16,0},{17,1},{18,2},{19,3},{20,4},{21,5},{22,6},{23,7},{24,8},{25... | collective-permute-start | bytes 221192 | tf_op jit(solution)/shard_map/ppermute | solution.py:44
  20.1 0.4 %collective-permute-start.9 = (f32[32,576]{1,0:T(8,128)S(1)}, f32[32,576]{1,0:T(8,128)S(1)}, u32[]{:S(2)}, u32[]{:S(2)}) collective-permute-start(f32[32,576]{1,0:T(8,128)S(1)} %get-tuple-element.35), channel_id=1, source_target_pairs={{8,0},{9,1},{10,2},{11,3},{12,4},{13,5},{14,6},{15,7},{0,8},{1,9},... | collective-permute-start | bytes 221192 | tf_op jit(solution)/shard_map/ppermute | solution.py:44
  20.5 2.2 %collective-permute-done.7.refs_1_ = f32[32,576]{1,0:T(8,128)S(1)} collective-permute-done((f32[32,576]{1,0:T(8,128)S(1)}, f32[32,576]{1,0:T(8,128)S(1)}, u32[]{:S(2)}, u32[]{:S(2)}) %collective-permute-start.7) | collective-permute-done | bytes 73760 | tf_op jit(solution)/shard_map/ppermute | solution.py:44
  22.7 1.7 %collective-permute-done.8.refs_2_ = f32[32,576]{1,0:T(8,128)S(1)} collective-permute-done((f32[32,576]{1,0:T(8,128)S(1)}, f32[32,576]{1,0:T(8,128)S(1)}, u32[]{:S(2)}, u32[]{:S(2)}) %collective-permute-start.8) | collective-permute-done | bytes 73760 | tf_op jit(solution)/shard_map/ppermute | solution.py:44
  24.4 0.2 collective-permute-done.9.refs_3_
  24.6 0.7 %shard_map.62 = (f32[32,64]{1,0:T(8,128)}, f32[32,512]{1,0:T(8,128)}) custom-call(f32[32,576]{1,0:T(8,128)S(1)} %get-tuple-element.32.refs_0_, f32[32,576]{1,0:T(8,128)S(1)} %collective-permute-done.7.refs_1_, f32[32,576]{1,0:T(8,128)S(1)} %collective-permute-done.8.refs_2_, f32[32,576]{1,0:T(8,128)S(1)} %collective-permute-done.9.refs_3_), custom_call_target="tpu_custom_call" | custom-call | tf_op jit(solution)/shard_map/pallas_call | solution.py:118
  (1 shorter events, 0.0 us)
Async XLA Ops:
  0.6 0.9 %copy-start = (f32[32,64]{1,0:T(8,128)S(1)}, f32[32,64]{1,0:T(8,128)}, u32[]{:S(2)}) copy-start(f32[32,64]{1,0:T(8,128)} %param.7) | copy-start | bytes 24580
  0.6 0.9 %copy-start.1 = (f32[32,64]{1,0:T(8,128)S(1)}, f32[32,64]{1,0:T(8,128)}, u32[]{:S(2)}) copy-start(f32[32,64]{1,0:T(8,128)} %param.6) | copy-start | bytes 24580
  1.6 1.4 %collective-permute-start = (f32[32,640]{1,0:T(8,128)S(1)}, f32[32,640]{1,0:T(8,128)S(1)}, u32[]{:S(2)}, u32[]{:S(2)}) collective-permute-start(f32[32,640]{1,0:T(8,128)S(1)} %pad_maximum_fusion.1.refs_0_), channel_id=1, source_target_pairs={{0,4},{4,0},{8,12},{12,8},{16,20},{20,16},{24,28},{28,24},{1,5},{5... | collective-permute-start | bytes 245768 | tf_op jit(solution)/shard_map/ppermute | solution.py:33
  3.1 7.1 %collective-permute-start.4 = (f32[64,640]{1,0:T(8,128)S(1)}, f32[64,640]{1,0:T(8,128)S(1)}, u32[]{:S(2)}, u32[]{:S(2)}) collective-permute-start(f32[64,640]{1,0:T(8,128)S(1)} %pad_maximum_fusion.refs_3_), channel_id=1, source_target_pairs={{0,24},{1,25},{2,26},{3,27},{4,7},{5,6},{6,5},{7,4},{8,16},{9,17},... | collective-permute-start | bytes 491528 | tf_op jit(solution)/shard_map/ppermute | solution.py:44
  6.9 5.3 %collective-permute-start.1 = (f32[64,640]{1,0:T(8,128)S(1)}, f32[64,640]{1,0:T(8,128)S(1)}, u32[]{:S(2)}, u32[]{:S(2)}) collective-permute-start(f32[64,640]{1,0:T(8,128)S(1)} %pad_maximum_fusion.refs_3_), channel_id=1, source_target_pairs={{0,16},{1,17},{2,18},{3,19},{4,12},{5,13},{6,14},{7,15},{8,24},{9,... | collective-permute-start | bytes 491528 | tf_op jit(solution)/shard_map/ppermute | solution.py:44
  7.4 7.2 %collective-permute-start.3 = (f32[64,640]{1,0:T(8,128)S(1)}, f32[64,640]{1,0:T(8,128)S(1)}, u32[]{:S(2)}, u32[]{:S(2)}) collective-permute-start(f32[64,640]{1,0:T(8,128)S(1)} %pad_maximum_fusion.refs_3_), channel_id=1, source_target_pairs={{0,1},{1,0},{2,3},{3,2},{4,6},{5,7},{6,4},{7,5},{8,9},{9,8},{10,11... | collective-permute-start | bytes 491528 | tf_op jit(solution)/shard_map/ppermute | solution.py:44
  10.2 3.4 %collective-permute-start.5 = (f32[64,640]{1,0:T(8,128)S(1)}, f32[64,640]{1,0:T(8,128)S(1)}, u32[]{:S(2)}, u32[]{:S(2)}) collective-permute-start(f32[64,640]{1,0:T(8,128)S(1)} %collective-permute-done.4.refs_4_), channel_id=1, source_target_pairs={{0,4},{4,0},{8,12},{12,8},{16,20},{20,16},{24,28},{28,24},{1,5},{5... | collective-permute-start | bytes 491528 | tf_op jit(solution)/shard_map/ppermute | solution.py:33
  12.2 1.4 %collective-permute-start.2 = (f32[32,640]{1,0:T(8,128)S(1)}, f32[32,640]{1,0:T(8,128)S(1)}, u32[]{:S(2)}, u32[]{:S(2)}) collective-permute-start(f32[32,640]{1,0:T(8,128)S(1)} %get-tuple-element.36), channel_id=1, source_target_pairs={{0,4},{4,0},{8,12},{12,8},{16,20},{20,16},{24,28},{28,24},{1,5},{5... | collective-permute-start | bytes 245768 | tf_op jit(solution)/shard_map/ppermute | solution.py:33
  14.6 1.5 %collective-permute-start.6 = (f32[64,640]{1,0:T(8,128)S(1)}, f32[64,640]{1,0:T(8,128)S(1)}, u32[]{:S(2)}, u32[]{:S(2)}) collective-permute-start(f32[64,640]{1,0:T(8,128)S(1)} %collective-permute-done.3.refs_3_), channel_id=1, source_target_pairs={{0,4},{4,0},{8,12},{12,8},{16,20},{20,16},{24,28},{28,24},{1,5},{5... | collective-permute-start | bytes 491528 | tf_op jit(solution)/shard_map/ppermute | solution.py:33
  16.9 5.7 %collective-permute-start.7 = (f32[32,576]{1,0:T(8,128)S(1)}, f32[32,576]{1,0:T(8,128)S(1)}, u32[]{:S(2)}, u32[]{:S(2)}) collective-permute-start(f32[32,576]{1,0:T(8,128)S(1)} %get-tuple-element.33), channel_id=1, source_target_pairs={{24,0},{25,1},{26,2},{27,3},{28,4},{29,5},{30,6},{31,7},{16,8},{17... | collective-permute-start | bytes 221192 | tf_op jit(solution)/shard_map/ppermute | solution.py:44
  19.5 4.9 %collective-permute-start.8 = (f32[32,576]{1,0:T(8,128)S(1)}, f32[32,576]{1,0:T(8,128)S(1)}, u32[]{:S(2)}, u32[]{:S(2)}) collective-permute-start(f32[32,576]{1,0:T(8,128)S(1)} %get-tuple-element.34), channel_id=1, source_target_pairs={{16,0},{17,1},{18,2},{19,3},{20,4},{21,5},{22,6},{23,7},{24,8},{25... | collective-permute-start | bytes 221192 | tf_op jit(solution)/shard_map/ppermute | solution.py:44
  20.1 4.4 %collective-permute-start.9 = (f32[32,576]{1,0:T(8,128)S(1)}, f32[32,576]{1,0:T(8,128)S(1)}, u32[]{:S(2)}, u32[]{:S(2)}) collective-permute-start(f32[32,576]{1,0:T(8,128)S(1)} %get-tuple-element.35), channel_id=1, source_target_pairs={{8,0},{9,1},{10,2},{11,3},{12,4},{13,5},{14,6},{15,7},{0,8},{1,9},... | collective-permute-start | bytes 221192 | tf_op jit(solution)/shard_map/ppermute | solution.py:44
